TPU v7x, 32 devices: a whole 2x2x4 slice. The times are simulated.
32 devices in a mesh: samp: 8 (over z, x), blk: 4 (over y, core).
Axes of the slice: x: 2, y: 2, z: 4, core: 2. Of those that a mesh axis runs over, the one named last changes fastest.
Arguments:
- dosages: bfloat16 [5120, 2048], P('samp', 'blk'), may hold values from 0 to 2
- traits: bfloat16 [16, 5120], P(None, 'samp'), may hold values from -6 to 6
- folds: int32 [5120], P('samp'), may hold values from 0 to 4
Outputs:
- level0: float32 [4, 5, 16, 5120], P(None, None, 'blk', 'samp')
- blend: float32 [16, 5120], P('blk', 'samp')
All inputs are finite; a program needn't handle non-finite values.
Results may differ from a plain program's by a relative error of at most 0.0097.
Values may be sent and summed in bfloat16 or wider, within the bound.
A program may use at most 64 MiB of HBM per device.

v0:
```python
import functools

import jax
import jax.numpy as jnp
from jax import lax
from jax.experimental import pallas as pl
from jax.experimental.pallas import tpu as pltpu
from jax.sharding import PartitionSpec as P

FOLDS = 5
SHRINK = 5


RATIOS = (99.0, 3.0, 1.0, 1.0 / 3.0, 1.0 / 99.0)
EPS = 1e-05
HIGH = lax.Precision.HIGHEST


def solve_batch(systems, right_sides):
    factors = jnp.linalg.cholesky(systems)

    def solve_single(factor, right_side):
        return jax.scipy.linalg.cho_solve((factor, True), right_side)

    return jax.vmap(solve_single)(factors, right_sides)


def shards(dosages, traits, folds):
    rows, width = dosages.shape
    traits_count = traits.shape[0]
    fold_ids = jnp.arange(FOLDS, dtype=jnp.int32)
    masks = (folds[None, :] == fold_ids[:, None]).astype(jnp.float32)
    mask_half = masks.astype(jnp.bfloat16)
    traits_wide = traits.astype(jnp.float32)
    grams = []
    crosses = []
    for fold in range(FOLDS):
        weighted = dosages * mask_half[fold][:, None]
        grams.append(jnp.einsum("ri,rj->ij", dosages, weighted, preferred_element_type=jnp.float32))
        crosses.append(
            jnp.dot(traits * mask_half[fold][None, :], dosages, preferred_element_type=jnp.float32)
        )
    gram = jnp.stack(grams)
    cross = jnp.stack(crosses)
    sums = jnp.dot(mask_half, dosages, preferred_element_type=jnp.float32)
    counts = jnp.sum(masks, axis=1)
    trait_sums = jnp.einsum("ks,ts->kt", masks, traits_wide, precision=HIGH)
    gram, sums, cross, counts, trait_sums = lax.psum(
        (gram, sums, cross, counts, trait_sums), "samp"
    )
    total = jnp.sum(counts)
    mean = jnp.sum(sums, axis=0) / total
    gram_total = jnp.sum(gram, axis=0)
    variance = jnp.diagonal(gram_total) / total - mean * mean
    scale = lax.rsqrt(variance + EPS)
    sums_total = jnp.sum(sums, axis=0)
    cross_total = jnp.sum(cross, axis=0)
    trait_total = jnp.sum(trait_sums, axis=0)
    ratios = jnp.array(RATIOS, dtype=jnp.float32)
    identity = jnp.eye(width, dtype=jnp.float32)

    def train_system(fold):
        train_gram = gram_total - lax.dynamic_index_in_dim(gram, fold, 0, keepdims=False)
        train_sums = sums_total - lax.dynamic_index_in_dim(sums, fold, 0, keepdims=False)
        train_count = total - lax.dynamic_index_in_dim(counts, fold, 0, keepdims=False)
        train_cross = cross_total - lax.dynamic_index_in_dim(cross, fold, 0, keepdims=False)
        train_traits = trait_total - lax.dynamic_index_in_dim(trait_sums, fold, 0, keepdims=False)
        centered = (
            train_gram
            - mean[:, None] * train_sums[None, :]
            - train_sums[:, None] * mean[None, :]
            + train_count * mean[:, None] * mean[None, :]
        )
        system = scale[:, None] * centered * scale[None, :]
        target = scale[:, None] * (train_cross.T - mean[:, None] * train_traits[None, :])
        return (system, target)

    systems_count = FOLDS * SHRINK
    per_device = -(-systems_count // lax.axis_size("samp"))
    first = lax.axis_index("samp") * per_device

    def solve_own(offset):
        which = jnp.minimum(first + offset, systems_count - 1)
        fold = which // SHRINK
        shrink = which - fold * SHRINK
        system, target = train_system(fold)
        penalty = jnp.sum(
            jnp.where(jnp.arange(SHRINK, dtype=jnp.int32) == shrink, ratios * width, 0.0)
        )
        beta = solve_batch((system + penalty * identity)[None], target[None])[0]
        return (scale[:, None] * beta).astype(jnp.bfloat16)

    owned = lax.map(solve_own, jnp.arange(per_device, dtype=jnp.int32))
    collected = lax.all_gather(owned, "samp", axis=0, tiled=True)
    coef = collected[:systems_count].reshape(FOLDS, SHRINK, width, traits_count)
    coef_flat = coef.transpose(2, 0, 1, 3).reshape(width, FOLDS * SHRINK * traits_count)
    shift = jnp.einsum("v,klvt->klt", mean, coef.astype(jnp.float32), precision=HIGH)
    raw = jnp.einsum("vc,rv->cr", coef_flat, dosages, preferred_element_type=jnp.float32)
    outcome = raw.reshape(FOLDS, SHRINK, traits_count, rows) - shift[..., None]
    level_pred = jnp.einsum("kltr,kr->ltr", outcome, masks, precision=HIGH)
    group = traits_count // lax.axis_size("blk")
    start = lax.axis_index("blk") * group
    own_traits = lax.dynamic_slice_in_dim(traits_wide, start, group, 0)
    own_sums = lax.dynamic_slice_in_dim(trait_sums, start, group, 1)
    arrived = lax.all_to_all(level_pred[None], "blk", split_axis=2, concat_axis=0, tiled=True)
    count_pred = arrived.shape[0] * arrived.shape[1]
    flat = arrived.reshape(count_pred, group, rows)
    raw_grams = jnp.einsum("ks,ats,bts->ktab", masks, flat, flat, precision=HIGH)
    raw_cross = jnp.einsum("ks,ats,ts->kta", masks, flat, own_traits, precision=HIGH)
    raw_sums = jnp.einsum("ks,ats->kta", masks, flat, precision=HIGH)
    raw_grams, raw_cross, raw_sums = lax.psum((raw_grams, raw_cross, raw_sums), "samp")
    pred_mean = jnp.sum(raw_sums, axis=0) / total
    pred_sq = jnp.diagonal(jnp.sum(raw_grams, axis=0), axis1=1, axis2=2)
    pred_scale = lax.rsqrt(pred_sq / total - pred_mean * pred_mean + EPS)
    standard = (flat - pred_mean.T[:, :, None]) * pred_scale.T[:, :, None]
    outer_scale = pred_scale[None, :, :, None] * pred_scale[None, :, None, :]
    fold_grams = outer_scale * (
        raw_grams
        - pred_mean[None, :, :, None] * raw_sums[:, :, None, :]
        - raw_sums[:, :, :, None] * pred_mean[None, :, None, :]
        + counts[:, None, None, None] * pred_mean[None, :, :, None] * pred_mean[None, :, None, :]
    )
    fold_cross = pred_scale[None] * (raw_cross - pred_mean[None] * own_sums[:, :, None])
    level0 = standard.reshape(arrived.shape)
    train_grams = jnp.sum(fold_grams, axis=0)[None] - fold_grams
    train_cross = jnp.sum(fold_cross, axis=0)[None] - fold_cross
    shrunk = train_grams + total / 4.0 * jnp.eye(count_pred, dtype=jnp.float32)
    weights = solve_batch(
        shrunk.reshape(-1, count_pred, count_pred), train_cross.reshape(-1, count_pred)
    )
    weights = weights.reshape(FOLDS, group, count_pred)
    every_fold = jnp.einsum("ats,kta->kts", standard, weights, precision=HIGH)
    blended = jnp.einsum("kts,ks->ts", every_fold, masks, precision=HIGH)
    blend_sum, blend_sq = lax.psum(
        (jnp.sum(blended, axis=-1), jnp.sum(blended * blended, axis=-1)), "samp"
    )
    blend_mean = blend_sum / total
    blend_var = blend_sq / total - blend_mean * blend_mean
    blend = (blended - blend_mean[:, None]) * lax.rsqrt(blend_var + EPS)[:, None]
    return (level0, blend)


MESH = pl.DeviceIdType.MESH
AUX = 32
ROWS1 = 24
PANEL = 128
LIMIT = 48 * 1024 * 1024
VMEM = pl.BlockSpec(memory_space=pltpu.VMEM)
ANY = pl.BlockSpec(memory_space=pl.ANY)


def high_dot(a, b, dims):
    return lax.dot_general(
        a, b, (dims, ((), ())), precision=HIGH, preferred_element_type=jnp.float32
    )


def greet(axis, count):
    barrier = pltpu.get_barrier_semaphore()
    me = lax.axis_index(axis)
    for step in range(1, count):
        pl.semaphore_signal(
            barrier, inc=1, device_id={axis: lax.rem(me + step, count)}, device_id_type=MESH
        )
    pl.semaphore_wait(barrier, count - 1)


def gather_kernel(depth, x_ref, aux_ref, xo_ref, auxo_ref, send, recv, asend, arecv, own):
    me = lax.axis_index("samp")
    z, x = me // 2, lax.rem(me, 2)
    greet("samp", 2 * depth)
    keep = pltpu.make_async_copy(x_ref, xo_ref.at[me], own.at[0])
    keep.start()
    keep_aux = pltpu.make_async_copy(aux_ref, auxo_ref.at[me], own.at[1])
    keep_aux.start()

    def x_copy(src, slot, lane, target):
        return pltpu.make_async_remote_copy(
            src_ref=src,
            dst_ref=xo_ref.at[slot],
            send_sem=send.at[lane],
            recv_sem=recv.at[slot],
            device_id={"samp": target},
            device_id_type=MESH,
        )

    def aux_copy(step):
        return pltpu.make_async_remote_copy(
            src_ref=aux_ref,
            dst_ref=auxo_ref.at[me],
            send_sem=asend.at[step],
            recv_sem=arecv.at[me],
            device_id={"samp": lax.rem(me + step, 2 * depth)},
            device_id_type=MESH,
        )

    partner = z * 2 + 1 - x
    for step in range(1, 2 * depth):
        aux_copy(step).start()

    @pl.when(z + 1 < depth)
    def _():
        x_copy(x_ref, me, 0, me + 2).start()

    @pl.when(z >= 1)
    def _():
        x_copy(x_ref, me, depth, me - 2).start()

    x_copy(x_ref, me, 2 * depth, partner).start()
    for far in range(1, depth):
        below, above = me - 2 * far, me + 2 * far

        @pl.when(z >= far)
        def _():
            x_copy(xo_ref.at[below], below, 0, partner).wait_recv()

            @pl.when(z + 1 < depth)
            def _():
                x_copy(xo_ref.at[below], below, far, me + 2).start()

            x_copy(xo_ref.at[below], below, 2 * depth + far, partner).start()

        @pl.when(z + far < depth)
        def _():
            x_copy(xo_ref.at[above], above, 0, partner).wait_recv()

            @pl.when(z >= 1)
            def _():
                x_copy(xo_ref.at[above], above, depth + far, me - 2).start()

            x_copy(xo_ref.at[above], above, 3 * depth + far, partner).start()

    for layer in range(depth):
        slot = layer * 2 + 1 - x
        x_copy(xo_ref.at[slot], slot, 0, partner).wait_recv()
    for step in range(1, 2 * depth):
        slot = lax.rem(me + step, 2 * depth)
        pltpu.make_async_remote_copy(
            src_ref=aux_ref,
            dst_ref=auxo_ref.at[slot],
            send_sem=asend.at[step],
            recv_sem=arecv.at[slot],
            device_id={"samp": slot},
            device_id_type=MESH,
        ).wait()
    x_copy(x_ref, me, 2 * depth, partner).wait_send()
    for far in range(depth):

        @pl.when((z >= far) & (z + 1 < depth))
        def _():
            x_copy(x_ref, me, far, partner).wait_send()

        @pl.when((z + far < depth) & (z >= 1))
        def _():
            x_copy(x_ref, me, depth + far, partner).wait_send()

        if far:

            @pl.when(z >= far)
            def _():
                x_copy(x_ref, me, 2 * depth + far, partner).wait_send()

            @pl.when(z + far < depth)
            def _():
                x_copy(x_ref, me, 3 * depth + far, partner).wait_send()

    keep.wait()
    keep_aux.wait()


def gather_samples(x, aux, count):
    return pl.pallas_call(
        functools.partial(gather_kernel, count // 2),
        out_shape=(
            jax.ShapeDtypeStruct((count,) + x.shape, x.dtype),
            jax.ShapeDtypeStruct((count,) + aux.shape, aux.dtype),
        ),
        in_specs=[ANY, ANY],
        out_specs=(ANY, ANY),
        scratch_shapes=[
            pltpu.SemaphoreType.DMA((2 * count,)),
            pltpu.SemaphoreType.DMA((count,)),
            pltpu.SemaphoreType.DMA((count,)),
            pltpu.SemaphoreType.DMA((count,)),
            pltpu.SemaphoreType.DMA((2,)),
        ],
        compiler_params=pltpu.CompilerParams(collective_id=0, has_side_effects=True),
        name="gather_samples",
    )(x, aux)


def spread_kernel(axis, count, split, a_ref, o_ref, send, recv, own):
    me = lax.axis_index(axis)
    greet(axis, count)
    keep = pltpu.make_async_copy(a_ref.at[me] if split else a_ref, o_ref.at[me], own)
    keep.start()
    for step in range(1, count):
        other = lax.rem(me + step, count)
        pltpu.make_async_remote_copy(
            src_ref=a_ref.at[other] if split else a_ref,
            dst_ref=o_ref.at[me],
            send_sem=send.at[step],
            recv_sem=recv.at[me],
            device_id={axis: other},
            device_id_type=MESH,
        ).start()
    for step in range(1, count):
        other = lax.rem(me + step, count)
        pltpu.make_async_remote_copy(
            src_ref=a_ref.at[other] if split else a_ref,
            dst_ref=o_ref.at[other],
            send_sem=send.at[step],
            recv_sem=recv.at[other],
            device_id={axis: other},
            device_id_type=MESH,
        ).wait()
    keep.wait()


def spread(a, axis, count, split, number):
    return pl.pallas_call(
        functools.partial(spread_kernel, axis, count, split),
        out_shape=jax.ShapeDtypeStruct(a.shape if split else (count,) + a.shape, a.dtype),
        in_specs=[VMEM],
        out_specs=VMEM,
        scratch_shapes=[
            pltpu.SemaphoreType.DMA((count,)),
            pltpu.SemaphoreType.DMA((count,)),
            pltpu.SemaphoreType.DMA,
        ],
        compiler_params=pltpu.CompilerParams(collective_id=number, has_side_effects=True),
        name="spread_" + axis + str(number),
    )(a)


def sweep(m_ref, batch, pivot):
    size, lanes = m_ref.shape[1:]
    row_at = lax.broadcasted_iota(jnp.int32, (size, lanes), 0) == pivot
    lane_at = lax.broadcasted_iota(jnp.int32, (size, lanes), 1) == pivot
    row_col = lax.broadcasted_iota(jnp.int32, (size, 1), 0) == pivot
    lane_row = lax.broadcasted_iota(jnp.int32, (1, lanes), 1) == pivot
    cross = row_at | lane_at
    rows = [m_ref[b, pl.ds(pivot, 1), :] for b in range(batch)]
    wholes = [m_ref[b] for b in range(batch)]
    heads = [jnp.sum(jnp.where(lane_row, row, 0.0), axis=1, keepdims=True) for row in rows]
    columns = [jnp.sum(jnp.where(lane_at, m, 0.0), axis=1, keepdims=True) for m in wholes]
    for b in range(batch):
        inverse = 1.0 / heads[b]
        row = jnp.where(lane_row, -inverse, rows[b] * inverse)
        column = jnp.where(row_col, -1.0, columns[b])
        m_ref[b] = jnp.where(cross, 0.0, wholes[b]) - column * row


def sweep_panel(m_ref, batch, step):
    size, lanes = m_ref.shape[1:]
    start = pl.multiple_of(step * 8, 8)
    sub = lax.broadcasted_iota(jnp.int32, (8, lanes), 0)
    lane = lax.broadcasted_iota(jnp.int32, (8, lanes), 1) - start
    inside = (lane >= 0) & (lane < 8)
    unit = jnp.where(lane == sub, 1.0, 0.0)
    panels = [m_ref[b, pl.ds(start, 8), :] for b in range(batch)]
    turned = [pltpu.roll(p, lanes - start, 1) for p in panels]
    columns = [
        [jnp.broadcast_to(p[:, j : j + 1], (8, lanes)) for j in range(8)] for p in turned
    ]
    solved = [jnp.where(inside, unit, p) for p in panels]
    for p in range(8):
        here = sub == p
        for b in range(batch):
            inverse = 1.0 / columns[b][p][p : p + 1]
            own = columns[b][p]
            line = solved[b][p : p + 1] * inverse
            solved[b] = jnp.where(here, line, solved[b] - own * line)
            for j in range(p + 1, 8):
                line = columns[b][j][p : p + 1] * inverse
                columns[b][j] = jnp.where(here, line, columns[b][j] - own * line)
    row = lax.broadcasted_iota(jnp.int32, (size, lanes), 0) - start
    col = lax.broadcasted_iota(jnp.int32, (size, lanes), 1) - start
    cross = ((row >= 0) & (row < 8)) | ((col >= 0) & (col < 8))
    for b in range(batch):
        left = jnp.where(inside, -unit, panels[b])
        right = jnp.where(inside, -solved[b], solved[b])
        m_ref[b] = jnp.where(cross, 0.0, m_ref[b]) - high_dot(left, right, ((0,), (0,)))


def solve_kernel(systems, own, x_ref, aux_ref, coef_ref, mean_ref, gram, cross, pairs, all_aux, sq, mats, rhs, diag):
    count, rows, width = x_ref.shape
    traits = coef_ref.shape[0] // own
    total = count * rows
    first = lax.axis_index("samp") * own
    fold_of = [jnp.minimum(first + i, systems - 1) // SHRINK for i in range(own)]
    folds = [fold_of[0], fold_of[own - 1]]
    for ref in (gram, cross, pairs, all_aux, sq):
        ref[...] = jnp.zeros_like(ref)
    aux_row = lax.broadcasted_iota(jnp.int32, (AUX, width), 0)
    fold_rows = (aux_row >= traits) & (aux_row < traits + FOLDS)
    picks = jnp.concatenate(
        [
            jnp.where(fold_rows & (aux_row != traits + fold), 1.0, 0.0).astype(jnp.bfloat16)
            for fold in folds
        ],
        axis=1,
    )
    row_id = lax.broadcasted_iota(jnp.int32, (AUX, rows), 0)

    def add_block(i, _):
        x = x_ref[i]
        aux = aux_ref[i]
        aux_wide = aux.astype(jnp.float32)
        keep = lax.dot_general(
            aux, picks, (((0,), (0,)), ((), ())), preferred_element_type=jnp.float32
        ).astype(jnp.bfloat16)
        weighted = jnp.concatenate([x, x], axis=1) * keep
        gram[...] += lax.dot_general(
            x, weighted, (((0,), (0,)), ((), ())), preferred_element_type=jnp.float32
        )
        all_aux[...] += jnp.dot(aux, x, preferred_element_type=jnp.float32)
        wide = x.astype(jnp.float32)
        sq[...] += jnp.sum(wide * wide, axis=0, keepdims=True)
        for j, fold in enumerate(folds):
            held = jnp.sum(jnp.where(row_id == traits + fold, aux_wide, 0.0), axis=0, keepdims=True)
            aux_train = (aux_wide * (1.0 - held)).astype(jnp.bfloat16)
            cross[j] += jnp.dot(aux_train, x, preferred_element_type=jnp.float32)
            pairs[j] += lax.dot_general(
                aux_train, aux, (((1,), (1,)), ((), ())), preferred_element_type=jnp.float32
            )
        return 0

    lax.fori_loop(0, count, add_block, 0)
    fold_lines = lambda a: jnp.sum(jnp.where(fold_rows, a, 0.0), axis=0, keepdims=True)
    mean = fold_lines(all_aux[...]) / total
    scale = lax.rsqrt(sq[...] / total - mean * mean + EPS)
    mean_ref[...] = jnp.broadcast_to(mean, mean_ref.shape)
    pair_row = lax.broadcasted_iota(jnp.int32, (AUX, AUX), 0)
    pair_col = lax.broadcasted_iota(jnp.int32, (AUX, AUX), 1)
    pair_fold = (pair_col >= traits) & (pair_col < traits + FOLDS)
    eye = lax.broadcasted_iota(jnp.int32, (width, width), 0) == lax.broadcasted_iota(
        jnp.int32, (width, width), 1
    )
    column_of = lambda line: jnp.sum(jnp.where(eye, line, 0.0), axis=1, keepdims=True)
    mean_col, scale_col = column_of(mean), column_of(scale)
    for j in range(2):
        sums = fold_lines(cross[j])
        pair = pairs[j]
        kept = jnp.sum(jnp.where(pair_fold & (pair_row == pair_col), pair, 0.0))
        trait_sums = jnp.sum(jnp.where(pair_fold, pair, 0.0), axis=1, keepdims=True)[:traits]
        half = slice(j * width, (j + 1) * width)
        gram[:, half] = scale_col * scale * (
            gram[:, half] - mean_col * sums - column_of(sums) * mean + kept * (mean_col * mean)
        )
        cross[j, :traits] = scale * (cross[j, :traits] - trait_sums * mean)
    for i in range(own):
        shrink = jnp.minimum(first + i, systems - 1) - fold_of[i] * SHRINK
        penalty = jnp.float32(RATIOS[0] * width)
        for l in range(1, SHRINK):
            penalty = jnp.where(shrink == l, jnp.float32(RATIOS[l] * width), penalty)
        late = fold_of[i] != folds[0]
        mats[i] = jnp.where(late, gram[:, width:], gram[:, :width]) + jnp.where(eye, penalty, 0.0)
        rhs[i] = jnp.where(late, cross[1, :traits], cross[0, :traits])
    steps = width // PANEL
    for j in range(steps):
        here = slice(j * PANEL, (j + 1) * PANEL)
        rest = slice((j + 1) * PANEL, width)
        at = diag.at[j]
        for i in range(own):
            at[i] = mats[i, here, here]

        def one(pivot, _):
            sweep_panel(at, own, pivot)
            return 0

        lax.fori_loop(0, PANEL // 8, one, 0)
        for i in range(own):
            right = -high_dot(rhs[i, :, here], at[i], ((1,), (0,)))
            rhs[i, :, here] = right
            if j + 1 < steps:
                tail = mats[i, here, rest]
                solved = high_dot(at[i], tail, ((1,), (0,)))
                mats[i, rest, rest] += high_dot(tail, solved, ((0,), (0,)))
                rhs[i, :, rest] -= high_dot(right, tail, ((1,), (0,)))
    for j in range(steps - 2, -1, -1):
        here = slice(j * PANEL, (j + 1) * PANEL)
        rest = slice((j + 1) * PANEL, width)
        for i in range(own):
            back = high_dot(rhs[i, :, rest], mats[i, here, rest], ((1,), (1,)))
            rhs[i, :, here] += high_dot(back, diag[j, i], ((1,), (0,)))
    for i in range(own):
        coef_ref[i * traits : (i + 1) * traits] = (rhs[i] * scale).astype(jnp.bfloat16)


def solve_level0(x_all, aux_all, traits):
    count, rows, width = x_all.shape
    systems = FOLDS * SHRINK
    own = -(-systems // count)
    f32 = jnp.float32
    return pl.pallas_call(
        functools.partial(solve_kernel, systems, own),
        out_shape=(
            jax.ShapeDtypeStruct((own * traits, width), jnp.bfloat16),
            jax.ShapeDtypeStruct((8, width), f32),
        ),
        in_specs=[VMEM, VMEM],
        out_specs=(VMEM, VMEM),
        scratch_shapes=[
            pltpu.VMEM((width, 2 * width), f32),
            pltpu.VMEM((2, AUX, width), f32),
            pltpu.VMEM((2, AUX, AUX), f32),
            pltpu.VMEM((AUX, width), f32),
            pltpu.VMEM((1, width), f32),
            pltpu.VMEM((own, width, width), f32),
            pltpu.VMEM((own, traits, width), f32),
            pltpu.VMEM((width // PANEL, own, PANEL, PANEL), f32),
        ],
        compiler_params=pltpu.CompilerParams(vmem_limit_bytes=LIMIT),
        name="solve_level0",
    )(x_all, aux_all)


def predict_kernel(coef_ref, mean_ref, x_ref, folds_ref, o_ref):
    parts, _, group, _ = o_ref.shape
    traits = parts * group
    per_fold = SHRINK * traits
    coef = coef_ref[: FOLDS * per_fold]
    raw = lax.dot_general(
        coef, x_ref[...], (((1,), (1,)), ((), ())), preferred_element_type=jnp.float32
    )
    shift = jnp.sum(coef.astype(jnp.float32) * mean_ref[:1], axis=1, keepdims=True)
    raw = raw - shift
    folds = folds_ref[...]
    out = jnp.zeros((per_fold, raw.shape[1]), jnp.float32)
    for k in range(FOLDS):
        out = jnp.where(folds == k, raw[k * per_fold : (k + 1) * per_fold], out)
    for g in range(parts):
        for l in range(SHRINK):
            o_ref[g, l] = out[l * traits + g * group : l * traits + (g + 1) * group]


def moments_kernel(p_ref, traits_ref, folds_ref, f_ref, e_ref):
    blocks, shrinks, group, rows = p_ref.shape
    preds = blocks * shrinks
    f_ref[...] = jnp.zeros_like(f_ref)
    for t in range(group):
        base = t * ROWS1
        for b in range(blocks):
            for l in range(shrinks):
                at = base + b * shrinks + l
                f_ref[at : at + 1] = p_ref[b, l, t : t + 1]
        f_ref[base + preds : base + preds + 1] = traits_ref[t : t + 1]
        f_ref[base + preds + 1 : base + preds + 2] = jnp.ones((1, rows), jnp.float32)
    f = f_ref[...]
    size = group * ROWS1
    folds = folds_ref[...]
    lane = lax.broadcasted_iota(jnp.int32, (ROWS1, size), 1)
    for k in range(FOLDS):
        full = high_dot(jnp.where(folds == k, f, 0.0), f, ((1,), (1,)))
        packed = jnp.zeros((ROWS1, size), jnp.float32)
        for t in range(group):
            inside = (lane >= t * ROWS1) & (lane < (t + 1) * ROWS1)
            packed = jnp.where(inside, full[t * ROWS1 : (t + 1) * ROWS1], packed)
        e_ref[k * ROWS1 : (k + 1) * ROWS1] = packed


def blend_kernel(total, e_ref, f_ref, p_ref, folds_ref, level_ref, blend_ref, mats):
    blocks, shrinks, group, rows = p_ref.shape
    preds = blocks * shrinks
    summed = jnp.sum(e_ref[...], axis=0)
    shape = (ROWS1, ROWS1)
    row = lax.broadcasted_iota(jnp.int32, shape, 0)
    col = lax.broadcasted_iota(jnp.int32, shape, 1)
    col_in = lax.broadcasted_iota(jnp.int32, (ROWS1, 1), 0) < preds
    row_in = lax.broadcasted_iota(jnp.int32, (1, ROWS1), 1) < preds
    one_lane = lax.broadcasted_iota(jnp.int32, (1, ROWS1), 1) == preds + 1
    ridge = jnp.where((row == col) & (row < preds), total / 4.0, 0.0)
    own = [
        [
            summed[k * ROWS1 : (k + 1) * ROWS1, t * ROWS1 : (t + 1) * ROWS1]
            for k in range(FOLDS)
        ]
        for t in range(group)
    ]
    means, scales = [], []
    for t in range(group):
        full = own[t][0]
        for k in range(1, FOLDS):
            full = full + own[t][k]
        mean_row = jnp.where(row_in, full[preds + 1 : preds + 2] / total, 0.0)
        mean_col = jnp.where(col_in, full[:, preds + 1 : preds + 2] / total, 0.0)
        square = jnp.where(row == col, full, 0.0) / total
        sq_row = jnp.sum(square, axis=0, keepdims=True)
        sq_col = jnp.sum(square, axis=1, keepdims=True)
        scale_row = jnp.where(row_in, lax.rsqrt(sq_row - mean_row * mean_row + EPS), 1.0)
        scale_col = jnp.where(col_in, lax.rsqrt(sq_col - mean_col * mean_col + EPS), 1.0)
        means.append((mean_row, mean_col))
        scales.append((scale_row, scale_col))
        for k in range(FOLDS):
            train = full - own[t][k]
            sums_row = train[preds + 1 : preds + 2]
            sums_col = train[:, preds + 1 : preds + 2]
            kept = train[preds + 1 : preds + 2, preds + 1 : preds + 2]
            centered = (
                train - mean_col * sums_row - sums_col * mean_row + kept * (mean_col * mean_row)
            )
            mats[t * FOLDS + k] = scale_col * scale_row * centered + ridge
    for b in range(blocks):
        for l in range(shrinks):
            at = b * shrinks + l
            means_at = jnp.concatenate([means[t][1][at : at + 1] for t in range(group)], axis=0)
            scales_at = jnp.concatenate([scales[t][1][at : at + 1] for t in range(group)], axis=0)
            level_ref[b, l] = (p_ref[b, l] - means_at) * scales_at

    def one(pivot, _):
        sweep(mats, group * FOLDS, pivot)
        return 0

    lax.fori_loop(0, preds, one, 0)
    folds = folds_ref[...]
    for t in range(group):
        mean_row, scale_row = means[t][0], scales[t][0]
        lines = []
        first = jnp.zeros((1, 1), jnp.float32)
        second = jnp.zeros((1, 1), jnp.float32)
        for k in range(FOLDS):
            line = jnp.where(row_in, mats[t * FOLDS + k, preds : preds + 1, :] * scale_row, 0.0)
            offset = jnp.sum(line * mean_row, axis=1, keepdims=True)
            line = jnp.where(one_lane, -offset, line)
            lines.append(line)
            product = jnp.sum(own[t][k] * line, axis=1, keepdims=True)
            line_col = jnp.sum(jnp.where(row == col, line, 0.0), axis=1, keepdims=True)
            first = first + product[preds + 1 : preds + 2]
            second = second + jnp.sum(product * line_col, axis=0, keepdims=True)
        lines.append(jnp.zeros((8 - FOLDS, ROWS1), jnp.float32))
        every = high_dot(
            jnp.concatenate(lines, axis=0),
            f_ref[t * ROWS1 : (t + 1) * ROWS1],
            ((1,), (0,)),
        )
        p = jnp.zeros((1, rows), jnp.float32)
        for k in range(FOLDS):
            p = jnp.where(folds == k, every[k : k + 1], p)
        mean = first / total
        spread_of = second / total - mean * mean
        blend_ref[t : t + 1] = (p - mean) * lax.rsqrt(spread_of + EPS)


def plain(kernel, out_shape, name, *args, scratch=()):
    return pl.pallas_call(
        kernel,
        out_shape=out_shape,
        in_specs=[VMEM] * len(args),
        out_specs=jax.tree.map(lambda _: VMEM, out_shape),
        scratch_shapes=list(scratch),
        compiler_params=pltpu.CompilerParams(vmem_limit_bytes=LIMIT),
        name=name,
    )(*args)


def fast(samp, blk, dosages, traits, folds):
    rows, width = dosages.shape
    count_traits = traits.shape[0]
    group = count_traits // blk
    f32 = jnp.float32
    fold_ids = jnp.arange(AUX - count_traits, dtype=jnp.int32)
    one_hot = (folds[None, :] == fold_ids[:, None]).astype(jnp.bfloat16)
    aux = jnp.concatenate([traits, one_hot], axis=0)
    folds_row = folds[None, :]
    own_traits = lax.dynamic_slice_in_dim(
        traits, lax.axis_index("blk") * group, group, 0
    ).astype(f32)
    x_all, aux_all = gather_samples(dosages, aux, samp)
    coef, mean = solve_level0(x_all, aux_all, count_traits)
    coef_all = spread(coef, "samp", samp, False, 1).reshape(-1, width)
    shape = jax.ShapeDtypeStruct((blk, SHRINK, group, rows), f32)
    pred = plain(predict_kernel, shape, "predict", coef_all, mean, dosages, folds_row)
    pred = spread(pred, "blk", blk, True, 2)
    size = group * ROWS1
    stacked, moments = plain(
        moments_kernel,
        (jax.ShapeDtypeStruct((size, rows), f32), jax.ShapeDtypeStruct((FOLDS * ROWS1, size), f32)),
        "moments",
        pred,
        own_traits,
        folds_row,
    )
    moments = spread(moments, "samp", samp, False, 3)
    level0, blend = plain(
        functools.partial(blend_kernel, float(samp * rows)),
        (shape, jax.ShapeDtypeStruct((group, rows), f32)),
        "blend",
        moments,
        stacked,
        pred,
        folds_row,
        scratch=[pltpu.VMEM((group * FOLDS, ROWS1, ROWS1), f32)],
    )
    return level0, blend


def solution(mesh):
    in_specs = (P("samp", "blk"), P(None, "samp"), P("samp"))
    out_specs = (P(None, None, "blk", "samp"), P("blk", "samp"))
    samp, blk = mesh.shape["samp"], mesh.shape["blk"]
    body = functools.partial(fast, samp, blk) if samp == 8 else shards
    return jax.shard_map(body, mesh=mesh, in_specs=in_specs, out_specs=out_specs, check_vma=False)
```

profile of v0, /device:TPU:0, one launch (start us, length us, event | category | flops | bytes accessed | tf_op | source)
XLA Modules:
  0.0 198.6 jit_solution(8074804558158111305)
XLA Ops:
  0.6 0.0 copy-start.10
  0.6 0.0 copy-start.1
  0.7 0.8 fusion
  1.4 1.3 pad_maximum_fusion.aux_ref
  2.8 73.8 %gather_samples.1 = (bf16[8,640,512]{2,1,0:T(8,128)(2,1)}, bf16[8,32,640]{2,1,0:T(8,128)(2,1)}) custom-call(bf16[640,512]{1,0:T(8,128)(2,1)} %x_ref.3, bf16[32,640]{1,0:T(8,128)(2,1)} %pad_maximum_fusion.aux_ref), custom_call_target="tpu_custom_call" | custom-call | tf_op jit(solution)/shard_map/gather_samples/pallas_call | solution.py:272
  76.6 0.0 copy-start
  76.6 2.5 %copy-done = bf16[8,640,512]{2,1,0:T(8,128)(2,1)S(1)} copy-done((bf16[8,640,512]{2,1,0:T(8,128)(2,1)S(1)}, bf16[8,640,512]{2,1,0:T(8,128)(2,1)}, u32[]{:S(2)}) %copy-start) | copy-done | bytes 5242904
  79.1 0.0 copy-start.7
  79.1 1.0 copy-done.7
  80.0 64.5 %solve_level0.1 = (bf16[64,512]{1,0:T(8,128)(2,1)S(1)}, f32[8,512]{1,0:T(8,128)S(1)}) custom-call(bf16[8,640,512]{2,1,0:T(8,128)(2,1)S(1)} %copy-done, bf16[8,32,640]{2,1,0:T(8,128)(2,1)S(1)} %copy-done.7), custom_call_target="tpu_custom_call" | custom-call | tf_op jit(solution)/shard_map/solve_level0/pallas_call | solution.py:496
  144.6 0.0 copy-start.8
  144.6 0.6 copy-done.8
  145.2 13.2 %spread_samp1.1 = bf16[8,64,512]{2,1,0:T(8,128)(2,1)} custom-call(bf16[64,512]{1,0:T(8,128)(2,1)} %copy-done.8), custom_call_target="tpu_custom_call" | custom-call | tf_op jit(solution)/shard_map/spread_samp1/pallas_call | solution.py:321
  158.4 0.0 copy-done.10
  158.5 0.0 copy-done.1
  158.5 0.0 copy-start.2
  158.5 1.0 copy-done.2
  159.5 0.5 predict.1.a_ref
  160.0 0.0 copy-start.6
  160.1 0.7 copy-done.6
  160.7 6.3 %spread_blk2.1.p_ref = f32[4,5,4,640]{3,2,1,0:T(4,128)} custom-call(f32[4,5,4,640]{3,2,1,0:T(4,128)} %copy-done.6), custom_call_target="tpu_custom_call" | custom-call | tf_op jit(solution)/shard_map/spread_blk2/pallas_call | solution.py:321
  167.1 0.7 dynamic-slice_convert_fusion.traits_ref
  167.8 0.0 copy-start.4
  167.8 0.9 copy-done.4
  168.7 1.4 moments.1
  170.1 0.0 copy-start.9
  170.1 0.6 copy-done.9
  170.7 16.0 %spread_samp3.1.e_ref = f32[8,120,96]{2,1,0:T(8,128)} custom-call(f32[120,96]{1,0:T(8,128)} %copy-done.9), custom_call_target="tpu_custom_call" | custom-call | tf_op jit(solution)/shard_map/spread_samp3/pallas_call | solution.py:321
  186.8 0.0 copy-start.3
  186.8 1.0 copy-done.3
  187.8 0.0 copy-start.5
  187.8 0.9 copy-done.5
  188.7 9.8 %blend.1 = (f32[4,5,4,640]{3,2,1,0:T(4,128)}, f32[4,640]{1,0:T(4,128)}) custom-call(f32[8,120,96]{2,1,0:T(8,128)S(1)} %copy-done.3, f32[96,640]{1,0:T(8,128)S(1)} %get-tuple-element.13.f_ref, f32[4,5,4,640]{3,2,1,0:T(4,128)S(1)} %copy-done.5, s32[1,640]{1,0:T(1,128)S(1)} %broadcast_in_dim.2.folds_ref), custom_call_target="tpu_custom_call" | custom-call | tf_op jit(solution)/shard_map/blend/pallas_call | solution.py:646
  (1 shorter events, 0.0 us)
Async XLA Ops:
  0.6 157.8 %copy-start.10 = (s32[640]{0:T(1024)S(1)}, s32[640]{0:T(1024)}, u32[]{:S(2)}) copy-start(s32[640]{0:T(1024)} %param.5) | copy-start | bytes 7684
  0.6 157.8 %copy-start.1 = (bf16[640,512]{1,0:T(8,128)(2,1)S(1)}, bf16[640,512]{1,0:T(8,128)(2,1)}, u32[]{:S(2)}) copy-start(bf16[640,512]{1,0:T(8,128)(2,1)} %x_ref.3) | copy-start | bytes 1966084
  76.6 2.5 %copy-start = (bf16[8,640,512]{2,1,0:T(8,128)(2,1)S(1)}, bf16[8,640,512]{2,1,0:T(8,128)(2,1)}, u32[]{:S(2)}) copy-start(bf16[8,640,512]{2,1,0:T(8,128)(2,1)} %get-tuple-element.8.x_ref) | copy-start | bytes 15728644
  79.1 1.0 copy-start.7
  144.6 0.6 copy-start.8
  158.5 1.0 copy-start.2
  160.0 0.7 copy-start.6
  167.8 0.9 copy-start.4
  170.1 0.6 copy-start.9
  186.8 1.0 copy-start.3
  187.8 0.9 copy-start.5
where the time goes:
time: 200 us; the launch traced here: 199 us
  Pallas kernels  186 us (93%)
  local copies, waits for them, and re-layouts  9.32 us (5%)
  other arithmetic  2.82 us (1%)
    pallas_call x1, Pallas kernels, gather_samples(): pl.pallas_call(functools.partial(gather_kernel, count // 2), out_shape=(j...  73.8 us
    pallas_call x1, Pallas kernels, solve_level0(): pl.pallas_call(functools.partial(solve_kernel, systems, own), out_shape=(...  64.5 us
    pallas_call x3, Pallas kernels, spread(): pl.pallas_call(functools.partial(spread_kernel, axis, count, split), out_...  35.5 us
    pallas_call x3, Pallas kernels, plain(): pl.pallas_call(kernel, out_shape=out_shape, in_specs=[VMEM] * len(args),...  11.8 us
    unnamed x22, local copies, waits for them, and re-layouts  9.31 us

commit v1 on v0

--- a/solution.py
+++ b/solution.py
@@ -165,172 +165,182 @@
     pl.semaphore_wait(barrier, count - 1)
 
 
-def gather_kernel(depth, x_ref, aux_ref, xo_ref, auxo_ref, send, recv, asend, arecv, own):
+def ranked(z, depth, rank):
+    near = jnp.minimum(z, depth - 1 - z)
+    both = jnp.where(lax.rem(rank, 2) == 1, z - (rank + 1) // 2, z + rank // 2)
+    one = jnp.where(z < depth - 1 - z, z + rank - near, z - rank + near)
+    return jnp.where(rank <= 2 * near, both, one)
+
+
+def gram_kernel(
+    depth, own_systems, traits, x_ref, aux_ref,
+    gram, cross, pairs, all_aux, sq,
+    xs, auxs, send_up, send_down, send_pair, recv, asend, arecv, own,
+):
     me = lax.axis_index("samp")
     z, x = me // 2, lax.rem(me, 2)
-    greet("samp", 2 * depth)
-    keep = pltpu.make_async_copy(x_ref, xo_ref.at[me], own.at[0])
+    partner = z * 2 + 1 - x
+    count = 2 * depth
+    keep = pltpu.make_async_copy(x_ref, xs.at[me], own.at[0])
     keep.start()
-    keep_aux = pltpu.make_async_copy(aux_ref, auxo_ref.at[me], own.at[1])
+    keep_aux = pltpu.make_async_copy(aux_ref, auxs.at[me], own.at[1])
     keep_aux.start()
-
-    def x_copy(src, slot, lane, target):
+    greet("samp", count)
+
+    def x_copy(slot, sem, target):
         return pltpu.make_async_remote_copy(
-            src_ref=src,
-            dst_ref=xo_ref.at[slot],
-            send_sem=send.at[lane],
+            src_ref=xs.at[slot],
+            dst_ref=xs.at[slot],
+            send_sem=sem,
             recv_sem=recv.at[slot],
             device_id={"samp": target},
             device_id_type=MESH,
         )
 
-    def aux_copy(step):
+    def aux_copy(step, slot):
+        other = lax.rem(me + step, count)
         return pltpu.make_async_remote_copy(
-            src_ref=aux_ref,
-            dst_ref=auxo_ref.at[me],
-            send_sem=asend.at[step],
-            recv_sem=arecv.at[me],
-            device_id={"samp": lax.rem(me + step, 2 * depth)},
-            device_id_type=MESH,
-        )
-
-    partner = z * 2 + 1 - x
-    for step in range(1, 2 * depth):
-        aux_copy(step).start()
-
-    @pl.when(z + 1 < depth)
-    def _():
-        x_copy(x_ref, me, 0, me + 2).start()
-
-    @pl.when(z >= 1)
-    def _():
-        x_copy(x_ref, me, depth, me - 2).start()
-
-    x_copy(x_ref, me, 2 * depth, partner).start()
-    for far in range(1, depth):
-        below, above = me - 2 * far, me + 2 * far
-
-        @pl.when(z >= far)
-        def _():
-            x_copy(xo_ref.at[below], below, 0, partner).wait_recv()
-
-            @pl.when(z + 1 < depth)
-            def _():
-                x_copy(xo_ref.at[below], below, far, me + 2).start()
-
-            x_copy(xo_ref.at[below], below, 2 * depth + far, partner).start()
-
-        @pl.when(z + far < depth)
-        def _():
-            x_copy(xo_ref.at[above], above, 0, partner).wait_recv()
-
-            @pl.when(z >= 1)
-            def _():
-                x_copy(xo_ref.at[above], above, depth + far, me - 2).start()
-
-            x_copy(xo_ref.at[above], above, 3 * depth + far, partner).start()
-
-    for layer in range(depth):
-        slot = layer * 2 + 1 - x
-        x_copy(xo_ref.at[slot], slot, 0, partner).wait_recv()
-    for step in range(1, 2 * depth):
-        slot = lax.rem(me + step, 2 * depth)
-        pltpu.make_async_remote_copy(
-            src_ref=aux_ref,
-            dst_ref=auxo_ref.at[slot],
+            src_ref=auxs.at[slot],
+            dst_ref=auxs.at[slot],
             send_sem=asend.at[step],
             recv_sem=arecv.at[slot],
-            device_id={"samp": slot},
+            device_id={"samp": other},
             device_id_type=MESH,
-        ).wait()
-    x_copy(x_ref, me, 2 * depth, partner).wait_send()
-    for far in range(depth):
-
-        @pl.when((z >= far) & (z + 1 < depth))
-        def _():
-            x_copy(x_ref, me, far, partner).wait_send()
-
-        @pl.when((z + far < depth) & (z >= 1))
-        def _():
-            x_copy(x_ref, me, depth + far, partner).wait_send()
-
-        if far:
-
-            @pl.when(z >= far)
-            def _():
-                x_copy(x_ref, me, 2 * depth + far, partner).wait_send()
-
-            @pl.when(z + far < depth)
-            def _():
-                x_copy(x_ref, me, 3 * depth + far, partner).wait_send()
+        )
 
     keep.wait()
     keep_aux.wait()
-
-
-def gather_samples(x, aux, count):
+    _, width = gram.shape
+    width = width // 2
+    rows = xs.shape[1]
+    folds = owned_folds(own_systems, FOLDS * SHRINK)
+    aux_row = lax.broadcasted_iota(jnp.int32, (AUX, width), 0)
+    fold_rows = (aux_row >= traits) & (aux_row < traits + FOLDS)
+    picks = jnp.concatenate(
+        [
+            jnp.where(fold_rows & (aux_row != traits + fold), 1.0, 0.0).astype(jnp.bfloat16)
+            for fold in folds
+        ],
+        axis=1,
+    )
+    row_id = lax.broadcasted_iota(jnp.int32, (AUX, rows), 0)
+
+    def forward(rank, layer, slot):
+        @pl.when((layer <= z) & (z + 1 < depth))
+        def _():
+            x_copy(slot, send_up.at[rank], me + 2).start()
+
+        @pl.when((layer >= z) & (z >= 1))
+        def _():
+            x_copy(slot, send_down.at[rank], me - 2).start()
+
+        x_copy(slot, send_pair.at[rank], partner).start()
+
+    forward(0, z, me)
+    for step in range(1, count):
+        aux_copy(step, me).start()
+    for ref in (gram, cross, pairs, all_aux, sq):
+        ref[...] = jnp.zeros_like(ref)
+
+    def add_block(i, _):
+        body = i < 2 * depth - 2
+        is_column = (i < 2) | (body & (lax.rem(i, 2) == 0))
+        column_rank = jnp.where(i < 2, i, i // 2 + 1)
+        pair_rank = jnp.where(body, (i - 3) // 2, i - depth)
+        rank = jnp.where(is_column, column_rank, pair_rank)
+        layer = ranked(z, depth, rank)
+        slot = layer * 2 + jnp.where(is_column, x, 1 - x)
+
+        @pl.when(i > 0)
+        def _():
+            x_copy(slot, send_pair.at[0], partner).wait_recv()
+
+            @pl.when(is_column)
+            def _():
+                forward(rank, layer, slot)
+
+            aux_copy(1, slot).wait_recv()
+
+        block = xs[slot]
+        aux = auxs[slot]
+        aux_wide = aux.astype(jnp.float32)
+        keep = lax.dot_general(
+            aux, picks, (((0,), (0,)), ((), ())), preferred_element_type=jnp.float32
+        ).astype(jnp.bfloat16)
+        weighted = jnp.concatenate([block, block], axis=1) * keep
+        gram[...] += lax.dot_general(
+            block, weighted, (((0,), (0,)), ((), ())), preferred_element_type=jnp.float32
+        )
+        all_aux[...] += jnp.dot(aux, block, preferred_element_type=jnp.float32)
+        wide = block.astype(jnp.float32)
+        sq[...] += jnp.sum(wide * wide, axis=0, keepdims=True)
+        for j, fold in enumerate(folds):
+            held = jnp.sum(jnp.where(row_id == traits + fold, aux_wide, 0.0), axis=0, keepdims=True)
+            aux_train = (aux_wide * (1.0 - held)).astype(jnp.bfloat16)
+            cross[j] += jnp.dot(aux_train, block, preferred_element_type=jnp.float32)
+            pairs[j] += lax.dot_general(
+                aux_train, aux, (((1,), (1,)), ((), ())), preferred_element_type=jnp.float32
+            )
+        return 0
+
+    lax.fori_loop(0, count, add_block, 0)
+    for step in range(1, count):
+        aux_copy(step, me).wait_send()
+    for rank in range(depth):
+        layer = ranked(z, depth, jnp.int32(rank))
+        slot = layer * 2 + x
+
+        @pl.when((layer <= z) & (z + 1 < depth))
+        def _():
+            x_copy(slot, send_up.at[rank], partner).wait_send()
+
+        @pl.when((layer >= z) & (z >= 1))
+        def _():
+            x_copy(slot, send_down.at[rank], partner).wait_send()
+
+        x_copy(slot, send_pair.at[rank], partner).wait_send()
+
+
+def owned_systems(count):
+    return -(-FOLDS * SHRINK // count)
+
+
+def owned_folds(own, systems):
+    first = lax.axis_index("samp") * own
+    return [jnp.minimum(first + i, systems - 1) // SHRINK for i in (0, own - 1)]
+
+
+def gather_grams(x, aux, count, traits):
+    rows, width = x.shape
+    f32 = jnp.float32
+    depth = count // 2
     return pl.pallas_call(
-        functools.partial(gather_kernel, count // 2),
+        functools.partial(gram_kernel, depth, owned_systems(count), traits),
         out_shape=(
-            jax.ShapeDtypeStruct((count,) + x.shape, x.dtype),
-            jax.ShapeDtypeStruct((count,) + aux.shape, aux.dtype),
+            jax.ShapeDtypeStruct((width, 2 * width), f32),
+            jax.ShapeDtypeStruct((2, AUX, width), f32),
+            jax.ShapeDtypeStruct((2, AUX, AUX), f32),
+            jax.ShapeDtypeStruct((AUX, width), f32),
+            jax.ShapeDtypeStruct((1, width), f32),
         ),
         in_specs=[ANY, ANY],
-        out_specs=(ANY, ANY),
+        out_specs=(VMEM,) * 5,
         scratch_shapes=[
-            pltpu.SemaphoreType.DMA((2 * count,)),
+            pltpu.VMEM((count, rows, width), x.dtype),
+            pltpu.VMEM((count, AUX, rows), aux.dtype),
+            pltpu.SemaphoreType.DMA((depth,)),
+            pltpu.SemaphoreType.DMA((depth,)),
+            pltpu.SemaphoreType.DMA((depth,)),
             pltpu.SemaphoreType.DMA((count,)),
             pltpu.SemaphoreType.DMA((count,)),
             pltpu.SemaphoreType.DMA((count,)),
             pltpu.SemaphoreType.DMA((2,)),
         ],
-        compiler_params=pltpu.CompilerParams(collective_id=0, has_side_effects=True),
-        name="gather_samples",
+        compiler_params=pltpu.CompilerParams(
+            collective_id=0, has_side_effects=True, vmem_limit_bytes=LIMIT
+        ),
+        name="gather_grams",
     )(x, aux)
-
-
-def spread_kernel(axis, count, split, a_ref, o_ref, send, recv, own):
-    me = lax.axis_index(axis)
-    greet(axis, count)
-    keep = pltpu.make_async_copy(a_ref.at[me] if split else a_ref, o_ref.at[me], own)
-    keep.start()
-    for step in range(1, count):
-        other = lax.rem(me + step, count)
-        pltpu.make_async_remote_copy(
-            src_ref=a_ref.at[other] if split else a_ref,
-            dst_ref=o_ref.at[me],
-            send_sem=send.at[step],
-            recv_sem=recv.at[me],
-            device_id={axis: other},
-            device_id_type=MESH,
-        ).start()
-    for step in range(1, count):
-        other = lax.rem(me + step, count)
-        pltpu.make_async_remote_copy(
-            src_ref=a_ref.at[other] if split else a_ref,
-            dst_ref=o_ref.at[other],
-            send_sem=send.at[step],
-            recv_sem=recv.at[other],
-            device_id={axis: other},
-            device_id_type=MESH,
-        ).wait()
-    keep.wait()
-
-
-def spread(a, axis, count, split, number):
-    return pl.pallas_call(
-        functools.partial(spread_kernel, axis, count, split),
-        out_shape=jax.ShapeDtypeStruct(a.shape if split else (count,) + a.shape, a.dtype),
-        in_specs=[VMEM],
-        out_specs=VMEM,
-        scratch_shapes=[
-            pltpu.SemaphoreType.DMA((count,)),
-            pltpu.SemaphoreType.DMA((count,)),
-            pltpu.SemaphoreType.DMA,
-        ],
-        compiler_params=pltpu.CompilerParams(collective_id=number, has_side_effects=True),
-        name="spread_" + axis + str(number),
-    )(a)
 
 
 def sweep(m_ref, batch, pivot):
@@ -383,50 +393,16 @@
         m_ref[b] = jnp.where(cross, 0.0, m_ref[b]) - high_dot(left, right, ((0,), (0,)))
 
 
-def solve_kernel(systems, own, x_ref, aux_ref, coef_ref, mean_ref, gram, cross, pairs, all_aux, sq, mats, rhs, diag):
-    count, rows, width = x_ref.shape
+def solve_kernel(
+    systems, own, total, gram, cross, pairs, all_aux, sq, coef_ref, mean_ref, mats, rhs, lines, diag
+):
+    width = gram.shape[0]
     traits = coef_ref.shape[0] // own
-    total = count * rows
     first = lax.axis_index("samp") * own
     fold_of = [jnp.minimum(first + i, systems - 1) // SHRINK for i in range(own)]
-    folds = [fold_of[0], fold_of[own - 1]]
-    for ref in (gram, cross, pairs, all_aux, sq):
-        ref[...] = jnp.zeros_like(ref)
+    folds = owned_folds(own, systems)
     aux_row = lax.broadcasted_iota(jnp.int32, (AUX, width), 0)
     fold_rows = (aux_row >= traits) & (aux_row < traits + FOLDS)
-    picks = jnp.concatenate(
-        [
-            jnp.where(fold_rows & (aux_row != traits + fold), 1.0, 0.0).astype(jnp.bfloat16)
-            for fold in folds
-        ],
-        axis=1,
-    )
-    row_id = lax.broadcasted_iota(jnp.int32, (AUX, rows), 0)
-
-    def add_block(i, _):
-        x = x_ref[i]
-        aux = aux_ref[i]
-        aux_wide = aux.astype(jnp.float32)
-        keep = lax.dot_general(
-            aux, picks, (((0,), (0,)), ((), ())), preferred_element_type=jnp.float32
-        ).astype(jnp.bfloat16)
-        weighted = jnp.concatenate([x, x], axis=1) * keep
-        gram[...] += lax.dot_general(
-            x, weighted, (((0,), (0,)), ((), ())), preferred_element_type=jnp.float32
-        )
-        all_aux[...] += jnp.dot(aux, x, preferred_element_type=jnp.float32)
-        wide = x.astype(jnp.float32)
-        sq[...] += jnp.sum(wide * wide, axis=0, keepdims=True)
-        for j, fold in enumerate(folds):
-            held = jnp.sum(jnp.where(row_id == traits + fold, aux_wide, 0.0), axis=0, keepdims=True)
-            aux_train = (aux_wide * (1.0 - held)).astype(jnp.bfloat16)
-            cross[j] += jnp.dot(aux_train, x, preferred_element_type=jnp.float32)
-            pairs[j] += lax.dot_general(
-                aux_train, aux, (((1,), (1,)), ((), ())), preferred_element_type=jnp.float32
-            )
-        return 0
-
-    lax.fori_loop(0, count, add_block, 0)
     fold_lines = lambda a: jnp.sum(jnp.where(fold_rows, a, 0.0), axis=0, keepdims=True)
     mean = fold_lines(all_aux[...]) / total
     scale = lax.rsqrt(sq[...] / total - mean * mean + EPS)
@@ -445,25 +421,25 @@
         kept = jnp.sum(jnp.where(pair_fold & (pair_row == pair_col), pair, 0.0))
         trait_sums = jnp.sum(jnp.where(pair_fold, pair, 0.0), axis=1, keepdims=True)[:traits]
         half = slice(j * width, (j + 1) * width)
-        gram[:, half] = scale_col * scale * (
+        mats[j] = scale_col * scale * (
             gram[:, half] - mean_col * sums - column_of(sums) * mean + kept * (mean_col * mean)
         )
-        cross[j, :traits] = scale * (cross[j, :traits] - trait_sums * mean)
-    for i in range(own):
+        lines[j] = scale * (cross[j, :traits] - trait_sums * mean)
+    for i in range(own - 1, -1, -1):
         shrink = jnp.minimum(first + i, systems - 1) - fold_of[i] * SHRINK
         penalty = jnp.float32(RATIOS[0] * width)
         for l in range(1, SHRINK):
             penalty = jnp.where(shrink == l, jnp.float32(RATIOS[l] * width), penalty)
-        late = fold_of[i] != folds[0]
-        mats[i] = jnp.where(late, gram[:, width:], gram[:, :width]) + jnp.where(eye, penalty, 0.0)
-        rhs[i] = jnp.where(late, cross[1, :traits], cross[0, :traits])
+        late = jnp.where(fold_of[i] != folds[0], 1, 0)
+        mats[i + 2] = mats[late] + jnp.where(eye, penalty, 0.0)
+        rhs[i] = lines[late]
     steps = width // PANEL
     for j in range(steps):
         here = slice(j * PANEL, (j + 1) * PANEL)
         rest = slice((j + 1) * PANEL, width)
         at = diag.at[j]
         for i in range(own):
-            at[i] = mats[i, here, here]
+            at[i] = mats[i + 2, here, here]
 
         def one(pivot, _):
             sweep_panel(at, own, pivot)
@@ -474,59 +450,51 @@
             right = -high_dot(rhs[i, :, here], at[i], ((1,), (0,)))
             rhs[i, :, here] = right
             if j + 1 < steps:
-                tail = mats[i, here, rest]
+                tail = mats[i + 2, here, rest]
                 solved = high_dot(at[i], tail, ((1,), (0,)))
-                mats[i, rest, rest] += high_dot(tail, solved, ((0,), (0,)))
+                mats[i + 2, rest, rest] += high_dot(tail, solved, ((0,), (0,)))
                 rhs[i, :, rest] -= high_dot(right, tail, ((1,), (0,)))
     for j in range(steps - 2, -1, -1):
         here = slice(j * PANEL, (j + 1) * PANEL)
         rest = slice((j + 1) * PANEL, width)
         for i in range(own):
-            back = high_dot(rhs[i, :, rest], mats[i, here, rest], ((1,), (1,)))
+            back = high_dot(rhs[i, :, rest], mats[i + 2, here, rest], ((1,), (1,)))
             rhs[i, :, here] += high_dot(back, diag[j, i], ((1,), (0,)))
     for i in range(own):
         coef_ref[i * traits : (i + 1) * traits] = (rhs[i] * scale).astype(jnp.bfloat16)
 
 
-def solve_level0(x_all, aux_all, traits):
-    count, rows, width = x_all.shape
-    systems = FOLDS * SHRINK
-    own = -(-systems // count)
+def solve_level0(sums, traits, count, rows):
+    width = sums[0].shape[0]
+    own = owned_systems(count)
     f32 = jnp.float32
-    return pl.pallas_call(
-        functools.partial(solve_kernel, systems, own),
-        out_shape=(
+    return plain(
+        functools.partial(solve_kernel, FOLDS * SHRINK, own, count * rows),
+        (
             jax.ShapeDtypeStruct((own * traits, width), jnp.bfloat16),
             jax.ShapeDtypeStruct((8, width), f32),
         ),
-        in_specs=[VMEM, VMEM],
-        out_specs=(VMEM, VMEM),
-        scratch_shapes=[
-            pltpu.VMEM((width, 2 * width), f32),
-            pltpu.VMEM((2, AUX, width), f32),
-            pltpu.VMEM((2, AUX, AUX), f32),
-            pltpu.VMEM((AUX, width), f32),
-            pltpu.VMEM((1, width), f32),
-            pltpu.VMEM((own, width, width), f32),
+        "solve_level0",
+        *sums,
+        scratch=[
+            pltpu.VMEM((own + 2, width, width), f32),
             pltpu.VMEM((own, traits, width), f32),
+            pltpu.VMEM((2, traits, width), f32),
             pltpu.VMEM((width // PANEL, own, PANEL, PANEL), f32),
         ],
-        compiler_params=pltpu.CompilerParams(vmem_limit_bytes=LIMIT),
-        name="solve_level0",
-    )(x_all, aux_all)
-
-
-def predict_kernel(coef_ref, mean_ref, x_ref, folds_ref, o_ref):
+    )
+
+
+def predict(coef, mean, x, folds, o_ref):
     parts, _, group, _ = o_ref.shape
     traits = parts * group
     per_fold = SHRINK * traits
-    coef = coef_ref[: FOLDS * per_fold]
+    coef = coef[: FOLDS * per_fold]
     raw = lax.dot_general(
-        coef, x_ref[...], (((1,), (1,)), ((), ())), preferred_element_type=jnp.float32
-    )
-    shift = jnp.sum(coef.astype(jnp.float32) * mean_ref[:1], axis=1, keepdims=True)
+        coef, x, (((1,), (1,)), ((), ())), preferred_element_type=jnp.float32
+    )
+    shift = jnp.sum(coef.astype(jnp.float32) * mean, axis=1, keepdims=True)
     raw = raw - shift
-    folds = folds_ref[...]
     out = jnp.zeros((per_fold, raw.shape[1]), jnp.float32)
     for k in range(FOLDS):
         out = jnp.where(folds == k, raw[k * per_fold : (k + 1) * per_fold], out)
@@ -535,7 +503,104 @@
             o_ref[g, l] = out[l * traits + g * group : l * traits + (g + 1) * group]
 
 
-def moments_kernel(p_ref, traits_ref, folds_ref, f_ref, e_ref):
+def level_kernel(
+    depth, blk, coef_ref, mean_ref, x_ref, traits_ref, folds_ref,
+    p_ref, f_ref, sum_ref,
+    coefs, sent, part, arrived,
+    send_line, send_pair, recv, send_blk, recv_blk, send_sum, recv_sum,
+):
+    count = 2 * depth
+    me = lax.axis_index("samp")
+    here = lax.axis_index("blk")
+    z, x = me // 2, lax.rem(me, 2)
+    partner = z * 2 + 1 - x
+    barrier = pltpu.get_barrier_semaphore()
+    for axis, size, at in (("samp", count, me), ("blk", blk, here)):
+        for step in range(1, size):
+            pl.semaphore_signal(
+                barrier,
+                inc=1,
+                device_id={axis: lax.rem(at + step, size)},
+                device_id_type=MESH,
+            )
+    coefs[me] = coef_ref[...]
+    pl.semaphore_wait(barrier, count + blk - 2)
+
+    def coef_copy(slot, sem, target):
+        return pltpu.make_async_remote_copy(
+            src_ref=coefs.at[slot],
+            dst_ref=coefs.at[slot],
+            send_sem=sem,
+            recv_sem=recv.at[slot],
+            device_id={"samp": target},
+            device_id_type=MESH,
+        )
+
+    mate = lambda step: lax.rem(z + step, depth) * 2 + x
+    for step in range(1, depth):
+        coef_copy(me, send_line.at[step], mate(step)).start()
+    coef_copy(me, send_pair.at[0], partner).start()
+    for step in range(1, depth):
+        coef_copy(mate(step), send_pair.at[0], partner).wait_recv()
+        coef_copy(mate(step), send_pair.at[step], partner).start()
+    for step in range(depth):
+        slot = lax.rem(z + step, depth) * 2 + 1 - x
+        coef_copy(slot, send_pair.at[0], partner).wait_recv()
+    predict(
+        coefs[...].reshape(-1, coefs.shape[2]),
+        mean_ref[:1],
+        x_ref[...],
+        folds_ref[...],
+        sent,
+    )
+
+    def pred_copy(step, slot):
+        other = lax.rem(here + step, blk)
+        return pltpu.make_async_remote_copy(
+            src_ref=sent.at[other],
+            dst_ref=p_ref.at[slot],
+            send_sem=send_blk.at[step],
+            recv_sem=recv_blk.at[slot],
+            device_id={"blk": other},
+            device_id_type=MESH,
+        )
+
+    for step in range(1, blk):
+        pred_copy(step, here).start()
+    p_ref[here] = sent[here]
+    for step in range(1, depth):
+        coef_copy(me, send_line.at[step], partner).wait_send()
+    for step in range(depth):
+        coef_copy(me, send_pair.at[step], partner).wait_send()
+    for step in range(1, blk):
+        pred_copy(step, lax.rem(here + step, blk)).wait()
+    moments(p_ref, traits_ref, folds_ref, f_ref, part.at[0])
+    stages = part.shape[0]
+    copies = []
+    for stage in range(stages):
+        bit = 2**stage
+        other = me + bit - 2 * bit * lax.rem(me // bit, 2)
+        copy = pltpu.make_async_remote_copy(
+            src_ref=part.at[stage],
+            dst_ref=arrived.at[stage],
+            send_sem=send_sum.at[stage],
+            recv_sem=recv_sum.at[stage],
+            device_id={"samp": other},
+            device_id_type=MESH,
+        )
+        copy.start()
+        copies.append(copy)
+        copy.wait_recv()
+        summed = part[stage] + arrived[stage]
+        if stage + 1 < stages:
+            part[stage + 1] = summed
+        else:
+            sum_ref[...] = summed
+    for copy in copies:
+        copy.wait_send()
+
+
+def moments(p_ref, traits_ref, folds_ref, f_ref, e_ref):
     blocks, shrinks, group, rows = p_ref.shape
     preds = blocks * shrinks
     f_ref[...] = jnp.zeros_like(f_ref)
@@ -563,7 +628,7 @@
 def blend_kernel(total, e_ref, f_ref, p_ref, folds_ref, level_ref, blend_ref, mats):
     blocks, shrinks, group, rows = p_ref.shape
     preds = blocks * shrinks
-    summed = jnp.sum(e_ref[...], axis=0)
+    summed = e_ref[...]
     shape = (ROWS1, ROWS1)
     row = lax.broadcasted_iota(jnp.int32, shape, 0)
     col = lax.broadcasted_iota(jnp.int32, shape, 1)
@@ -666,27 +731,46 @@
     own_traits = lax.dynamic_slice_in_dim(
         traits, lax.axis_index("blk") * group, group, 0
     ).astype(f32)
-    x_all, aux_all = gather_samples(dosages, aux, samp)
-    coef, mean = solve_level0(x_all, aux_all, count_traits)
-    coef_all = spread(coef, "samp", samp, False, 1).reshape(-1, width)
+    sums = gather_grams(dosages, aux, samp, count_traits)
+    coef, mean = solve_level0(sums, count_traits, samp, rows)
     shape = jax.ShapeDtypeStruct((blk, SHRINK, group, rows), f32)
-    pred = plain(predict_kernel, shape, "predict", coef_all, mean, dosages, folds_row)
-    pred = spread(pred, "blk", blk, True, 2)
     size = group * ROWS1
-    stacked, moments = plain(
-        moments_kernel,
-        (jax.ShapeDtypeStruct((size, rows), f32), jax.ShapeDtypeStruct((FOLDS * ROWS1, size), f32)),
-        "moments",
-        pred,
-        own_traits,
-        folds_row,
-    )
-    moments = spread(moments, "samp", samp, False, 3)
+    own = owned_systems(samp) * count_traits
+    depth = samp // 2
+    stages = samp.bit_length() - 1
+    dma = pltpu.SemaphoreType.DMA
+    pred, stacked, moment_sums = pl.pallas_call(
+        functools.partial(level_kernel, depth, blk),
+        out_shape=(
+            shape,
+            jax.ShapeDtypeStruct((size, rows), f32),
+            jax.ShapeDtypeStruct((FOLDS * ROWS1, size), f32),
+        ),
+        in_specs=[VMEM] * 5,
+        out_specs=(VMEM,) * 3,
+        scratch_shapes=[
+            pltpu.VMEM((samp, own, width), jnp.bfloat16),
+            pltpu.VMEM(shape.shape, f32),
+            pltpu.VMEM((stages, FOLDS * ROWS1, size), f32),
+            pltpu.VMEM((stages, FOLDS * ROWS1, size), f32),
+            dma((depth,)),
+            dma((depth,)),
+            dma((samp,)),
+            dma((blk,)),
+            dma((blk,)),
+            dma((stages,)),
+            dma((stages,)),
+        ],
+        compiler_params=pltpu.CompilerParams(
+            collective_id=1, has_side_effects=True, vmem_limit_bytes=LIMIT
+        ),
+        name="predict_level0",
+    )(coef, mean, dosages, own_traits, folds_row)
     level0, blend = plain(
         functools.partial(blend_kernel, float(samp * rows)),
         (shape, jax.ShapeDtypeStruct((group, rows), f32)),
         "blend",
-        moments,
+        moment_sums,
         stacked,
         pred,
         folds_row,

time: 200 us -> 170 us (0.85)
  Pallas kernels: 186 us -> 166 us
  local copies, waits for them, and re-layouts: 9.32 us -> 1.1 us
    pallas_call x5 -> x2, Pallas kernels: 174 us -> 103 us  [the longest x1 70.3 us: gather_grams(): pl.pallas_call(functools.partial(gram_kernel, depth, owned_systems(count)...]
    pallas_call x3 -> x2, Pallas kernels: 11.8 us -> 62.6 us  [plain(): pl.pallas_call(kernel, out_shape=out_shape, in_specs=[VMEM] * len(args),...]
    unnamed x22 -> x6, local copies, waits for them, and re-layouts: 9.31 us -> 1.09 us
where the time goes in v1:
time: 170 us
  Pallas kernels  166 us (98%)
  other arithmetic  2.21 us (1%)
    pallas_call x1, Pallas kernels, gather_grams(): pl.pallas_call(functools.partial(gram_kernel, depth, owned_systems(count)...  70.3 us
    pallas_call x2, Pallas kernels, plain(): pl.pallas_call(kernel, out_shape=out_shape, in_specs=[VMEM] * len(args),...  62.6 us
    pallas_call x1, Pallas kernels, fast(): pl.pallas_call(functools.partial(level_kernel, depth, blk), out_shape=(sh...  32.6 us

profile of v1, /device:TPU:0, one launch (start us, length us, event | category | flops | bytes accessed | tf_op | source)
XLA Modules:
  0.0 169.5 jit_solution(6550288776694550978)
XLA Ops:
  0.6 0.0 copy-start.2
  0.6 0.8 fusion
  1.4 0.7 pad_maximum_fusion.aux_ref
  2.1 0.0 copy-start
  2.1 1.1 copy-done
  3.2 0.0 copy-start.1
  3.2 70.3 %gather_grams.1 = (f32[512,1024]{1,0:T(8,128)S(1)}, f32[2,32,512]{2,1,0:T(8,128)S(1)}, f32[2,32,32]{2,1,0:T(8,128)S(1)}, f32[32,512]{1,0:T(8,128)S(1)}, f32[1,512]{1,0:T(1,128)S(1)}) custom-call(bf16[640,512]{1,0:T(8,128)(2,1)S(1)} %copy-done, bf16[32,640]{1,0:T(8,128)(2,1)S(1)} %pad_maximum_fusion.aux_ref), custom_call_target="tpu_custom_call" | custom-call | tf_op jit(solution)/shard_map/gather_grams/pallas_call | solution.py:317
  73.6 52.7 %solve_level0.1 = (bf16[64,512]{1,0:T(8,128)(2,1)S(1)}, f32[8,512]{1,0:T(8,128)S(1)}) custom-call(f32[512,1024]{1,0:T(8,128)S(1)} %get-tuple-element.12.gram, f32[2,32,512]{2,1,0:T(8,128)S(1)} %get-tuple-element.13.cross, f32[2,32,32]{2,1,0:T(8,128)S(1)} %get-tuple-element.14.pairs, f32[32,512]{1,0:T(8,128)S(1)} %get-tuple-element.15.all_aux, ...), custom_call_target="tpu_custom_call" | custom-call | tf_op jit(solution)/shard_map/solve_level0/pallas_call | solution.py:711
  126.3 0.7 dynamic-slice_convert_fusion.traits_ref
  127.0 0.0 copy-done.2
  127.0 0.0 copy-done.1
  127.0 32.6 %predict_level0.1 = (f32[4,5,4,640]{3,2,1,0:T(4,128)S(1)}, f32[96,640]{1,0:T(8,128)S(1)}, f32[120,96]{1,0:T(8,128)S(1)}) custom-call(bf16[64,512]{1,0:T(8,128)(2,1)S(1)} %get-tuple-element.17.coef_ref, f32[8,512]{1,0:T(8,128)S(1)} %get-tuple-element.18.mean_ref, bf16[640,512]{1,0:T(8,128)(2,1)S(1)} %copy-done.1, ...), custom_call_target="tpu_custom_call" | custom-call | tf_op jit(solution)/shard_map/predict_level0/pallas_call | solution.py:742
  159.6 9.9 %blend.1 = (f32[4,5,4,640]{3,2,1,0:T(4,128)}, f32[4,640]{1,0:T(4,128)}) custom-call(f32[120,96]{1,0:T(8,128)S(1)} %get-tuple-element.19.e_ref, f32[96,640]{1,0:T(8,128)S(1)} %get-tuple-element.20.f_ref, f32[4,5,4,640]{3,2,1,0:T(4,128)S(1)} %get-tuple-element.21.p_ref, s32[1,640]{1,0:T(1,128)S(1)} %broadcast_in_dim.2.folds_ref), custom_call_target="tpu_custom_call" | custom-call | tf_op jit(solution)/shard_map/blend/pallas_call | solution.py:711
  (1 shorter events, 0.0 us)
Async XLA Ops:
  0.6 126.4 %copy-start.2 = (s32[640]{0:T(1024)S(1)}, s32[640]{0:T(1024)}, u32[]{:S(2)}) copy-start(s32[640]{0:T(1024)} %param.5) | copy-start | bytes 7684
  2.1 1.1 copy-start
  3.2 123.8 %copy-start.1 = (bf16[640,512]{1,0:T(8,128)(2,1)S(1)}, bf16[640,512]{1,0:T(8,128)(2,1)}, u32[]{:S(2)}) copy-start(bf16[640,512]{1,0:T(8,128)(2,1)} %x_ref.3) | copy-start | bytes 1966084

commit v2 on v1

--- a/solution.py
+++ b/solution.py
@@ -343,54 +343,68 @@
     )(x, aux)
 
 
-def sweep(m_ref, batch, pivot):
+def split_three(a):
+    high = a.astype(jnp.bfloat16).astype(jnp.float32)
+    rest = a - high
+    middle = rest.astype(jnp.bfloat16).astype(jnp.float32)
+    return high, middle, rest - middle
+
+
+def thin_product(left, right):
+    a, b, c = split_three(left)
+    d, e, f = split_three(right)
+    return lax.dot_general(
+        jnp.concatenate([c, a, b, a, b, a], axis=0).astype(jnp.bfloat16),
+        jnp.concatenate([d, f, e, e, d, d], axis=0).astype(jnp.bfloat16),
+        (((0,), (0,)), ((), ())),
+        preferred_element_type=jnp.float32,
+    )
+
+
+def sweep_panel(m_ref, batch, start, pivots):
     size, lanes = m_ref.shape[1:]
-    row_at = lax.broadcasted_iota(jnp.int32, (size, lanes), 0) == pivot
-    lane_at = lax.broadcasted_iota(jnp.int32, (size, lanes), 1) == pivot
-    row_col = lax.broadcasted_iota(jnp.int32, (size, 1), 0) == pivot
-    lane_row = lax.broadcasted_iota(jnp.int32, (1, lanes), 1) == pivot
-    cross = row_at | lane_at
-    rows = [m_ref[b, pl.ds(pivot, 1), :] for b in range(batch)]
-    wholes = [m_ref[b] for b in range(batch)]
-    heads = [jnp.sum(jnp.where(lane_row, row, 0.0), axis=1, keepdims=True) for row in rows]
-    columns = [jnp.sum(jnp.where(lane_at, m, 0.0), axis=1, keepdims=True) for m in wholes]
-    for b in range(batch):
-        inverse = 1.0 / heads[b]
-        row = jnp.where(lane_row, -inverse, rows[b] * inverse)
-        column = jnp.where(row_col, -1.0, columns[b])
-        m_ref[b] = jnp.where(cross, 0.0, wholes[b]) - column * row
-
-
-def sweep_panel(m_ref, batch, step):
-    size, lanes = m_ref.shape[1:]
-    start = pl.multiple_of(step * 8, 8)
     sub = lax.broadcasted_iota(jnp.int32, (8, lanes), 0)
     lane = lax.broadcasted_iota(jnp.int32, (8, lanes), 1) - start
-    inside = (lane >= 0) & (lane < 8)
+    inside = (lane >= 0) & (lane < pivots)
     unit = jnp.where(lane == sub, 1.0, 0.0)
     panels = [m_ref[b, pl.ds(start, 8), :] for b in range(batch)]
-    turned = [pltpu.roll(p, lanes - start, 1) for p in panels]
+    if isinstance(start, int):
+        turned, first = panels, start
+    else:
+        turned, first = [pltpu.roll(p, lanes - start, 1) for p in panels], 0
     columns = [
-        [jnp.broadcast_to(p[:, j : j + 1], (8, lanes)) for j in range(8)] for p in turned
+        [jnp.broadcast_to(p[:, first + j : first + j + 1], (8, lanes)) for j in range(pivots)]
+        for p in turned
     ]
     solved = [jnp.where(inside, unit, p) for p in panels]
-    for p in range(8):
-        here = sub == p
+    for p in range(0, pivots, 2):
+        q = p + 1
+        at_p, at_q = sub == p, sub == q
         for b in range(batch):
-            inverse = 1.0 / columns[b][p][p : p + 1]
-            own = columns[b][p]
-            line = solved[b][p : p + 1] * inverse
-            solved[b] = jnp.where(here, line, solved[b] - own * line)
-            for j in range(p + 1, 8):
-                line = columns[b][j][p : p + 1] * inverse
-                columns[b][j] = jnp.where(here, line, columns[b][j] - own * line)
+            one, two = columns[b][p], columns[b][q]
+            pp, pq = one[p : p + 1], two[p : p + 1]
+            qp, qq = one[q : q + 1], two[q : q + 1]
+            inverse = 1.0 / (pp * qq - pq * qp)
+
+            def eliminate(t):
+                tp, tq = t[p : p + 1], t[q : q + 1]
+                up = (qq * tp - pq * tq) * inverse
+                uq = (pp * tq - qp * tp) * inverse
+                return jnp.where(at_p, up, jnp.where(at_q, uq, t - one * up - two * uq))
+
+            solved[b] = eliminate(solved[b])
+            for j in range(q + 1, pivots):
+                columns[b][j] = eliminate(columns[b][j])
     row = lax.broadcasted_iota(jnp.int32, (size, lanes), 0) - start
     col = lax.broadcasted_iota(jnp.int32, (size, lanes), 1) - start
-    cross = ((row >= 0) & (row < 8)) | ((col >= 0) & (col < 8))
+    cross = ((row >= 0) & (row < pivots)) | ((col >= 0) & (col < pivots))
     for b in range(batch):
         left = jnp.where(inside, -unit, panels[b])
         right = jnp.where(inside, -solved[b], solved[b])
-        m_ref[b] = jnp.where(cross, 0.0, m_ref[b]) - high_dot(left, right, ((0,), (0,)))
+        if pivots < 8:
+            left = jnp.where(sub < pivots, left, 0.0)
+            right = jnp.where(sub < pivots, right, 0.0)
+        m_ref[b] = jnp.where(cross, 0.0, m_ref[b]) - thin_product(left, right)
 
 
 def solve_kernel(
@@ -441,8 +455,8 @@
         for i in range(own):
             at[i] = mats[i + 2, here, here]
 
-        def one(pivot, _):
-            sweep_panel(at, own, pivot)
+        def one(step, _):
+            sweep_panel(at, own, pl.multiple_of(step * 8, 8), 8)
             return 0
 
         lax.fori_loop(0, PANEL // 8, one, 0)
@@ -673,11 +687,8 @@
             scales_at = jnp.concatenate([scales[t][1][at : at + 1] for t in range(group)], axis=0)
             level_ref[b, l] = (p_ref[b, l] - means_at) * scales_at
 
-    def one(pivot, _):
-        sweep(mats, group * FOLDS, pivot)
-        return 0
-
-    lax.fori_loop(0, preds, one, 0)
+    for start in range(0, preds, 8):
+        sweep_panel(mats, group * FOLDS, start, min(8, preds - start))
     folds = folds_ref[...]
     for t in range(group):
         mean_row, scale_row = means[t][0], scales[t][0]

time: 170 us -> 165 us (0.971)
  Pallas kernels: 166 us -> 161 us
    pallas_call x2, Pallas kernels: 62.6 us -> 58.1 us  [plain(): pl.pallas_call(kernel, out_shape=out_shape, in_specs=[VMEM] * len(args),...]
where the time goes in v2:
time: 165 us
  Pallas kernels  161 us (98%)
  other arithmetic  2.21 us (1%)
    pallas_call x1, Pallas kernels, gather_grams(): pl.pallas_call(functools.partial(gram_kernel, depth, owned_systems(count)...  70.3 us
    pallas_call x2, Pallas kernels, plain(): pl.pallas_call(kernel, out_shape=out_shape, in_specs=[VMEM] * len(args),...  58.1 us
    pallas_call x1, Pallas kernels, fast(): pl.pallas_call(functools.partial(level_kernel, depth, blk), out_shape=(sh...  32.6 us

profile of v2, /device:TPU:0, one launch (start us, length us, event | category | flops | bytes accessed | tf_op | source)
XLA Modules:
  0.0 165.0 jit_solution(6781607551226086045)
XLA Ops:
  0.6 0.0 copy-start.2
  0.6 0.8 fusion
  1.4 0.7 pad_maximum_fusion.aux_ref
  2.1 0.0 copy-start
  2.1 1.1 copy-done
  3.2 0.0 copy-start.1
  3.2 70.3 %gather_grams.1 = (f32[512,1024]{1,0:T(8,128)S(1)}, f32[2,32,512]{2,1,0:T(8,128)S(1)}, f32[2,32,32]{2,1,0:T(8,128)S(1)}, f32[32,512]{1,0:T(8,128)S(1)}, f32[1,512]{1,0:T(1,128)S(1)}) custom-call(bf16[640,512]{1,0:T(8,128)(2,1)S(1)} %copy-done, bf16[32,640]{1,0:T(8,128)(2,1)S(1)} %pad_maximum_fusion.aux_ref), custom_call_target="tpu_custom_call" | custom-call | tf_op jit(solution)/shard_map/gather_grams/pallas_call | solution.py:317
  73.6 47.8 %solve_level0.1 = (bf16[64,512]{1,0:T(8,128)(2,1)S(1)}, f32[8,512]{1,0:T(8,128)S(1)}) custom-call(f32[512,1024]{1,0:T(8,128)S(1)} %get-tuple-element.12.gram, f32[2,32,512]{2,1,0:T(8,128)S(1)} %get-tuple-element.13.cross, f32[2,32,32]{2,1,0:T(8,128)S(1)} %get-tuple-element.14.pairs, f32[32,512]{1,0:T(8,128)S(1)} %get-tuple-element.15.all_aux, ...), custom_call_target="tpu_custom_call" | custom-call | tf_op jit(solution)/shard_map/solve_level0/pallas_call | solution.py:722
  121.3 0.7 dynamic-slice_convert_fusion.traits_ref
  122.1 0.0 copy-done.2
  122.1 0.0 copy-done.1
  122.1 32.6 %predict_level0.1 = (f32[4,5,4,640]{3,2,1,0:T(4,128)S(1)}, f32[96,640]{1,0:T(8,128)S(1)}, f32[120,96]{1,0:T(8,128)S(1)}) custom-call(bf16[64,512]{1,0:T(8,128)(2,1)S(1)} %get-tuple-element.17.coef_ref, f32[8,512]{1,0:T(8,128)S(1)} %get-tuple-element.18.mean_ref, bf16[640,512]{1,0:T(8,128)(2,1)S(1)} %copy-done.1, ...), custom_call_target="tpu_custom_call" | custom-call | tf_op jit(solution)/shard_map/predict_level0/pallas_call | solution.py:753
  154.7 10.3 %blend.1 = (f32[4,5,4,640]{3,2,1,0:T(4,128)}, f32[4,640]{1,0:T(4,128)}) custom-call(f32[120,96]{1,0:T(8,128)S(1)} %get-tuple-element.19.e_ref, f32[96,640]{1,0:T(8,128)S(1)} %get-tuple-element.20.f_ref, f32[4,5,4,640]{3,2,1,0:T(4,128)S(1)} %get-tuple-element.21.p_ref, s32[1,640]{1,0:T(1,128)S(1)} %broadcast_in_dim.2.folds_ref), custom_call_target="tpu_custom_call" | custom-call | tf_op jit(solution)/shard_map/blend/pallas_call | solution.py:722
  (1 shorter events, 0.0 us)
Async XLA Ops:
  0.6 121.4 %copy-start.2 = (s32[640]{0:T(1024)S(1)}, s32[640]{0:T(1024)}, u32[]{:S(2)}) copy-start(s32[640]{0:T(1024)} %param.5) | copy-start | bytes 7684
  2.1 1.1 copy-start
  3.2 118.9 %copy-start.1 = (bf16[640,512]{1,0:T(8,128)(2,1)S(1)}, bf16[640,512]{1,0:T(8,128)(2,1)}, u32[]{:S(2)}) copy-start(bf16[640,512]{1,0:T(8,128)(2,1)} %x_ref.3) | copy-start | bytes 1966084

commit v3 on v2

--- a/solution.py
+++ b/solution.py
@@ -175,12 +175,17 @@
 def gram_kernel(
     depth, own_systems, traits, x_ref, aux_ref,
     gram, cross, pairs, all_aux, sq,
-    xs, auxs, send_up, send_down, send_pair, recv, asend, arecv, own,
+    xs, auxs, send_up, send_down, send_pair, recv, asend, arecv, own, send_extra, recv_half,
 ):
     me = lax.axis_index("samp")
     z, x = me // 2, lax.rem(me, 2)
     partner = z * 2 + 1 - x
     count = 2 * depth
+    is_end = (z == 0) | (z == depth - 1)
+    is_middle = (z > 0) & (z < depth - 1)
+    far = jnp.where(z < depth // 2, depth - 1, 0)
+    near = depth - 1 - far
+    half = xs.shape[1] // 2
     keep = pltpu.make_async_copy(x_ref, xs.at[me], own.at[0])
     keep.start()
     keep_aux = pltpu.make_async_copy(aux_ref, auxs.at[me], own.at[1])
@@ -196,6 +201,38 @@
             device_id={"samp": target},
             device_id_type=MESH,
         )
+
+    def half_copy(slot, part, send_sem, recv_sem, target):
+        piece = xs.at[slot, pl.ds(part * half, half)]
+        return pltpu.make_async_remote_copy(
+            src_ref=piece,
+            dst_ref=piece,
+            send_sem=send_sem,
+            recv_sem=recv_sem,
+            device_id={"samp": target},
+            device_id_type=MESH,
+        )
+
+    def to_pair(rank, layer, slot, act):
+        @pl.when((is_end & (layer != far)) | (is_middle & (layer != near)))
+        def _():
+            act(x_copy(slot, send_pair.at[rank], partner))
+
+        @pl.when(is_end & (layer == far))
+        def _():
+            act(half_copy(slot, 1, send_pair.at[rank], recv.at[slot], partner))
+
+    def extra(act):
+        target = jnp.where((z == 0) | ((z != depth - 1) & (z >= depth // 2)), me + 2, me - 2)
+
+        @pl.when(is_end)
+        def _():
+            act(x_copy(partner, send_extra.at[0], target))
+
+        @pl.when(is_middle)
+        def _():
+            slot = far * 2 + 1 - x
+            act(half_copy(slot, 0, send_extra.at[0], recv_half.at[0], target))
 
     def aux_copy(step, slot):
         other = lax.rem(me + step, count)
@@ -234,7 +271,7 @@
         def _():
             x_copy(slot, send_down.at[rank], me - 2).start()
 
-        x_copy(slot, send_pair.at[rank], partner).start()
+        to_pair(rank, layer, slot, lambda copy: copy.start())
 
     forward(0, z, me)
     for step in range(1, count):
@@ -244,6 +281,9 @@
 
     def add_block(i, _):
         body = i < 2 * depth - 2
+        swap = is_end & (i >= 2) & body
+        i_first = i
+        i = jnp.where(swap, i + 1 - 2 * lax.rem(i, 2), i)
         is_column = (i < 2) | (body & (lax.rem(i, 2) == 0))
         column_rank = jnp.where(i < 2, i, i // 2 + 1)
         pair_rank = jnp.where(body, (i - 3) // 2, i - depth)
@@ -251,13 +291,26 @@
         layer = ranked(z, depth, rank)
         slot = layer * 2 + jnp.where(is_column, x, 1 - x)
 
-        @pl.when(i > 0)
+        @pl.when(i_first > 0)
         def _():
-            x_copy(slot, send_pair.at[0], partner).wait_recv()
+            cut = is_end & jnp.logical_not(is_column) & (layer == far)
+
+            @pl.when(jnp.logical_not(cut))
+            def _():
+                x_copy(slot, send_pair.at[0], partner).wait_recv()
+
+            @pl.when(cut)
+            def _():
+                half_copy(slot, 1, send_pair.at[0], recv.at[slot], partner).wait_recv()
+                half_copy(slot, 0, send_pair.at[0], recv_half.at[0], partner).wait_recv()
 
             @pl.when(is_column)
             def _():
                 forward(rank, layer, slot)
+
+            @pl.when(jnp.logical_not(is_column) & (layer == jnp.where(is_end, z, far)))
+            def _():
+                extra(lambda copy: copy.start())
 
             aux_copy(1, slot).wait_recv()
 
@@ -298,7 +351,8 @@
         def _():
             x_copy(slot, send_down.at[rank], partner).wait_send()
 
-        x_copy(slot, send_pair.at[rank], partner).wait_send()
+        to_pair(rank, layer, slot, lambda copy: copy.wait_send())
+    extra(lambda copy: copy.wait_send())
 
 
 def owned_systems(count):
@@ -335,6 +389,8 @@
             pltpu.SemaphoreType.DMA((count,)),
             pltpu.SemaphoreType.DMA((count,)),
             pltpu.SemaphoreType.DMA((2,)),
+            pltpu.SemaphoreType.DMA((1,)),
+            pltpu.SemaphoreType.DMA((1,)),
         ],
         compiler_params=pltpu.CompilerParams(
             collective_id=0, has_side_effects=True, vmem_limit_bytes=LIMIT

time: 165 us -> 159 us (0.964)
  Pallas kernels: 161 us -> 154 us
    pallas_call x1, Pallas kernels: 70.3 us -> 65.8 us  [gather_grams(): pl.pallas_call(functools.partial(gram_kernel, depth, owned_systems(count)...]
    pallas_call x1, Pallas kernels: 32.6 us -> 30.4 us  [fast(): pl.pallas_call(functools.partial(level_kernel, depth, blk), out_shape=(sh...]
where the time goes in v3:
time: 159 us; the launch traced here: 158 us
  Pallas kernels  154 us (97%)
  other arithmetic  2.21 us (1%)
    pallas_call x1, Pallas kernels, gather_grams(): pl.pallas_call(functools.partial(gram_kernel, depth, owned_systems(count)...  65.8 us
    pallas_call x2, Pallas kernels, plain(): pl.pallas_call(kernel, out_shape=out_shape, in_specs=[VMEM] * len(args),...  58.1 us
    pallas_call x1, Pallas kernels, fast(): pl.pallas_call(functools.partial(level_kernel, depth, blk), out_shape=(sh...  30.4 us

profile of v3, /device:TPU:0, one launch (start us, length us, event | category | flops | bytes accessed | tf_op | source)
XLA Modules:
  0.0 158.2 jit_solution(13402064713391681214)
XLA Ops:
  0.6 0.0 copy-start.2
  0.6 0.8 fusion
  1.4 0.7 pad_maximum_fusion.aux_ref
  2.1 0.0 copy-start
  2.1 1.1 copy-done
  3.2 0.0 copy-start.1
  3.2 65.8 %gather_grams.1 = (f32[512,1024]{1,0:T(8,128)S(1)}, f32[2,32,512]{2,1,0:T(8,128)S(1)}, f32[2,32,32]{2,1,0:T(8,128)S(1)}, f32[32,512]{1,0:T(8,128)S(1)}, f32[1,512]{1,0:T(1,128)S(1)}) custom-call(bf16[640,512]{1,0:T(8,128)(2,1)S(1)} %copy-done, bf16[32,640]{1,0:T(8,128)(2,1)S(1)} %pad_maximum_fusion.aux_ref), custom_call_target="tpu_custom_call" | custom-call | tf_op jit(solution)/shard_map/gather_grams/pallas_call | solution.py:371
  69.0 47.8 %solve_level0.1 = (bf16[64,512]{1,0:T(8,128)(2,1)S(1)}, f32[8,512]{1,0:T(8,128)S(1)}) custom-call(f32[512,1024]{1,0:T(8,128)S(1)} %get-tuple-element.12.gram, f32[2,32,512]{2,1,0:T(8,128)S(1)} %get-tuple-element.13.cross, f32[2,32,32]{2,1,0:T(8,128)S(1)} %get-tuple-element.14.pairs, f32[32,512]{1,0:T(8,128)S(1)} %get-tuple-element.15.all_aux, ...), custom_call_target="tpu_custom_call" | custom-call | tf_op jit(solution)/shard_map/solve_level0/pallas_call | solution.py:778
  116.8 0.7 dynamic-slice_convert_fusion.traits_ref
  117.5 0.0 copy-done.2
  117.5 0.0 copy-done.1
  117.5 30.4 %predict_level0.1 = (f32[4,5,4,640]{3,2,1,0:T(4,128)S(1)}, f32[96,640]{1,0:T(8,128)S(1)}, f32[120,96]{1,0:T(8,128)S(1)}) custom-call(bf16[64,512]{1,0:T(8,128)(2,1)S(1)} %get-tuple-element.17.coef_ref, f32[8,512]{1,0:T(8,128)S(1)} %get-tuple-element.18.mean_ref, bf16[640,512]{1,0:T(8,128)(2,1)S(1)} %copy-done.1, ...), custom_call_target="tpu_custom_call" | custom-call | tf_op jit(solution)/shard_map/predict_level0/pallas_call | solution.py:809
  147.9 10.3 %blend.1 = (f32[4,5,4,640]{3,2,1,0:T(4,128)}, f32[4,640]{1,0:T(4,128)}) custom-call(f32[120,96]{1,0:T(8,128)S(1)} %get-tuple-element.19.e_ref, f32[96,640]{1,0:T(8,128)S(1)} %get-tuple-element.20.f_ref, f32[4,5,4,640]{3,2,1,0:T(4,128)S(1)} %get-tuple-element.21.p_ref, s32[1,640]{1,0:T(1,128)S(1)} %broadcast_in_dim.2.folds_ref), custom_call_target="tpu_custom_call" | custom-call | tf_op jit(solution)/shard_map/blend/pallas_call | solution.py:778
  (1 shorter events, 0.0 us)
Async XLA Ops:
  0.6 116.9 %copy-start.2 = (s32[640]{0:T(1024)S(1)}, s32[640]{0:T(1024)}, u32[]{:S(2)}) copy-start(s32[640]{0:T(1024)} %param.5) | copy-start | bytes 7684
  2.1 1.1 copy-start
  3.2 114.3 %copy-start.1 = (bf16[640,512]{1,0:T(8,128)(2,1)S(1)}, bf16[640,512]{1,0:T(8,128)(2,1)}, u32[]{:S(2)}) copy-start(bf16[640,512]{1,0:T(8,128)(2,1)} %x_ref.3) | copy-start | bytes 1966084

commit v4 on v3

--- a/solution.py
+++ b/solution.py
@@ -146,7 +146,7 @@
 PANEL = 128
 LIMIT = 48 * 1024 * 1024
 VMEM = pl.BlockSpec(memory_space=pltpu.VMEM)
-ANY = pl.BlockSpec(memory_space=pl.ANY)
+HBM = pl.BlockSpec(memory_space=pltpu.HBM)
 
 
 def high_dot(a, b, dims):
@@ -173,7 +173,7 @@
 
 
 def gram_kernel(
-    depth, own_systems, traits, x_ref, aux_ref,
+    depth, own_systems, x_ref, traits_ref, folds_ref,
     gram, cross, pairs, all_aux, sq,
     xs, auxs, send_up, send_down, send_pair, recv, asend, arecv, own, send_extra, recv_half,
 ):
@@ -186,10 +186,12 @@
     far = jnp.where(z < depth // 2, depth - 1, 0)
     near = depth - 1 - far
     half = xs.shape[1] // 2
-    keep = pltpu.make_async_copy(x_ref, xs.at[me], own.at[0])
+    keep = pltpu.make_async_copy(x_ref, xs.at[me], own)
     keep.start()
-    keep_aux = pltpu.make_async_copy(aux_ref, auxs.at[me], own.at[1])
-    keep_aux.start()
+    traits = traits_ref.shape[0]
+    fold_id = lax.broadcasted_iota(jnp.int32, (AUX - traits, xs.shape[1]), 0)
+    auxs[me, :traits] = traits_ref[...]
+    auxs[me, traits:] = jnp.where(folds_ref[...] == fold_id, 1.0, 0.0).astype(jnp.bfloat16)
     greet("samp", count)
 
     def x_copy(slot, sem, target):
@@ -246,7 +248,6 @@
         )
 
     keep.wait()
-    keep_aux.wait()
     _, width = gram.shape
     width = width // 2
     rows = xs.shape[1]
@@ -364,12 +365,12 @@
     return [jnp.minimum(first + i, systems - 1) // SHRINK for i in (0, own - 1)]
 
 
-def gather_grams(x, aux, count, traits):
+def gather_grams(x, traits, folds, count):
     rows, width = x.shape
     f32 = jnp.float32
     depth = count // 2
     return pl.pallas_call(
-        functools.partial(gram_kernel, depth, owned_systems(count), traits),
+        functools.partial(gram_kernel, depth, owned_systems(count)),
         out_shape=(
             jax.ShapeDtypeStruct((width, 2 * width), f32),
             jax.ShapeDtypeStruct((2, AUX, width), f32),
@@ -377,18 +378,18 @@
             jax.ShapeDtypeStruct((AUX, width), f32),
             jax.ShapeDtypeStruct((1, width), f32),
         ),
-        in_specs=[ANY, ANY],
+        in_specs=[HBM, VMEM, VMEM],
         out_specs=(VMEM,) * 5,
         scratch_shapes=[
             pltpu.VMEM((count, rows, width), x.dtype),
-            pltpu.VMEM((count, AUX, rows), aux.dtype),
+            pltpu.VMEM((count, AUX, rows), traits.dtype),
             pltpu.SemaphoreType.DMA((depth,)),
             pltpu.SemaphoreType.DMA((depth,)),
             pltpu.SemaphoreType.DMA((depth,)),
             pltpu.SemaphoreType.DMA((count,)),
             pltpu.SemaphoreType.DMA((count,)),
             pltpu.SemaphoreType.DMA((count,)),
-            pltpu.SemaphoreType.DMA((2,)),
+            pltpu.SemaphoreType.DMA,
             pltpu.SemaphoreType.DMA((1,)),
             pltpu.SemaphoreType.DMA((1,)),
         ],
@@ -396,7 +397,7 @@
             collective_id=0, has_side_effects=True, vmem_limit_bytes=LIMIT
         ),
         name="gather_grams",
-    )(x, aux)
+    )(x, traits, folds)
 
 
 def split_three(a):
@@ -522,7 +523,11 @@
             if j + 1 < steps:
                 tail = mats[i + 2, here, rest]
                 solved = high_dot(at[i], tail, ((1,), (0,)))
-                mats[i + 2, rest, rest] += high_dot(tail, solved, ((0,), (0,)))
+                for at_row in range((j + 1) * PANEL, width, PANEL):
+                    lead = at_row - (j + 1) * PANEL
+                    mats[i + 2, at_row : at_row + PANEL, at_row:] += high_dot(
+                        tail[:, lead : lead + PANEL], solved[:, lead:], ((0,), (0,))
+                    )
                 rhs[i, :, rest] -= high_dot(right, tail, ((1,), (0,)))
     for j in range(steps - 2, -1, -1):
         here = slice(j * PANEL, (j + 1) * PANEL)
@@ -644,7 +649,7 @@
         coef_copy(me, send_pair.at[step], partner).wait_send()
     for step in range(1, blk):
         pred_copy(step, lax.rem(here + step, blk)).wait()
-    moments(p_ref, traits_ref, folds_ref, f_ref, part.at[0])
+    moments(here * p_ref.shape[2], p_ref, traits_ref, folds_ref, f_ref, part.at[0])
     stages = part.shape[0]
     copies = []
     for stage in range(stages):
@@ -670,17 +675,21 @@
         copy.wait_send()
 
 
-def moments(p_ref, traits_ref, folds_ref, f_ref, e_ref):
+def moments(first, p_ref, traits_ref, folds_ref, f_ref, e_ref):
     blocks, shrinks, group, rows = p_ref.shape
     preds = blocks * shrinks
     f_ref[...] = jnp.zeros_like(f_ref)
+    traits = traits_ref[...].astype(jnp.float32)
+    trait_id = lax.broadcasted_iota(jnp.int32, traits.shape, 0) - first
     for t in range(group):
         base = t * ROWS1
         for b in range(blocks):
             for l in range(shrinks):
                 at = base + b * shrinks + l
                 f_ref[at : at + 1] = p_ref[b, l, t : t + 1]
-        f_ref[base + preds : base + preds + 1] = traits_ref[t : t + 1]
+        f_ref[base + preds : base + preds + 1] = jnp.sum(
+            jnp.where(trait_id == t, traits, 0.0), axis=0, keepdims=True
+        )
         f_ref[base + preds + 1 : base + preds + 2] = jnp.ones((1, rows), jnp.float32)
     f = f_ref[...]
     size = group * ROWS1
@@ -791,14 +800,8 @@
     count_traits = traits.shape[0]
     group = count_traits // blk
     f32 = jnp.float32
-    fold_ids = jnp.arange(AUX - count_traits, dtype=jnp.int32)
-    one_hot = (folds[None, :] == fold_ids[:, None]).astype(jnp.bfloat16)
-    aux = jnp.concatenate([traits, one_hot], axis=0)
     folds_row = folds[None, :]
-    own_traits = lax.dynamic_slice_in_dim(
-        traits, lax.axis_index("blk") * group, group, 0
-    ).astype(f32)
-    sums = gather_grams(dosages, aux, samp, count_traits)
+    sums = gather_grams(dosages, traits, folds_row, samp)
     coef, mean = solve_level0(sums, count_traits, samp, rows)
     shape = jax.ShapeDtypeStruct((blk, SHRINK, group, rows), f32)
     size = group * ROWS1
@@ -832,7 +835,7 @@
             collective_id=1, has_side_effects=True, vmem_limit_bytes=LIMIT
         ),
         name="predict_level0",
-    )(coef, mean, dosages, own_traits, folds_row)
+    )(coef, mean, dosages, traits, folds_row)
     level0, blend = plain(
         functools.partial(blend_kernel, float(samp * rows)),
         (shape, jax.ShapeDtypeStruct((group, rows), f32)),

time: 159 us -> 157 us (0.987)
  other arithmetic: 2.21 us -> 0 us
where the time goes in v4:
time: 157 us
  Pallas kernels  154 us (98%)
  local copies, waits for them, and re-layouts  2.51 us (2%)
    pallas_call x1, Pallas kernels, gather_grams(): pl.pallas_call(functools.partial(gram_kernel, depth, owned_systems(count)...  65.7 us
    pallas_call x2, Pallas kernels, plain(): pl.pallas_call(kernel, out_shape=out_shape, in_specs=[VMEM] * len(args),...  57.8 us
    pallas_call x1, Pallas kernels, fast(): pl.pallas_call(functools.partial(level_kernel, depth, blk), out_shape=(sh...  30.3 us

profile of v4, /device:TPU:0, one launch (start us, length us, event | category | flops | bytes accessed | tf_op | source)
XLA Modules:
  0.0 157.0 jit_solution(15428203260296429579)
XLA Ops:
  0.6 0.7 broadcast_in_dim.3.folds_ref
  1.3 0.0 copy-start
  1.3 1.1 copy-done
  2.4 0.0 copy-start.2
  2.4 0.7 copy-done.2
  3.1 0.0 copy-start.1
  3.1 65.7 %gather_grams.1 = (f32[512,1024]{1,0:T(8,128)S(1)}, f32[2,32,512]{2,1,0:T(8,128)S(1)}, f32[2,32,32]{2,1,0:T(8,128)S(1)}, f32[32,512]{1,0:T(8,128)S(1)}, f32[1,512]{1,0:T(1,128)S(1)}) custom-call(bf16[640,512]{1,0:T(8,128)(2,1)S(1)} %copy-done, bf16[16,640]{1,0:T(8,128)(2,1)S(1)} %copy-done.2, s32[1,640]{1,0:T(1,128)S(1)} %broadcast_in_dim.3.folds_ref), custom_call_target="tpu_custom_call" | custom-call | tf_op jit(solution)/shard_map/gather_grams/pallas_call | solution.py:372
  68.9 47.5 %solve_level0.1 = (bf16[64,512]{1,0:T(8,128)(2,1)S(1)}, f32[8,512]{1,0:T(8,128)S(1)}) custom-call(f32[512,1024]{1,0:T(8,128)S(1)} %get-tuple-element.12.gram, f32[2,32,512]{2,1,0:T(8,128)S(1)} %get-tuple-element.13.cross, f32[2,32,32]{2,1,0:T(8,128)S(1)} %get-tuple-element.14.pairs, f32[32,512]{1,0:T(8,128)S(1)} %get-tuple-element.15.all_aux, ...), custom_call_target="tpu_custom_call" | custom-call | tf_op jit(solution)/shard_map/solve_level0/pallas_call | solution.py:787
  116.3 0.0 copy-done.1
  116.3 30.3 %predict_level0.1 = (f32[4,5,4,640]{3,2,1,0:T(4,128)S(1)}, f32[96,640]{1,0:T(8,128)S(1)}, f32[120,96]{1,0:T(8,128)S(1)}) custom-call(bf16[64,512]{1,0:T(8,128)(2,1)S(1)} %get-tuple-element.17.coef_ref, f32[8,512]{1,0:T(8,128)S(1)} %get-tuple-element.18.mean_ref, bf16[640,512]{1,0:T(8,128)(2,1)S(1)} %copy-done.1, bf16[16,640]{1,0:T(8,128)(2,1)S(1)} %copy-done.2, ...), custom_call_target="tpu_custom_call" | custom-call | tf_op jit(solution)/shard_map/predict_level0/pallas_call | solution.py:812
  146.7 10.3 %blend.1 = (f32[4,5,4,640]{3,2,1,0:T(4,128)}, f32[4,640]{1,0:T(4,128)}) custom-call(f32[120,96]{1,0:T(8,128)S(1)} %get-tuple-element.19.e_ref, f32[96,640]{1,0:T(8,128)S(1)} %get-tuple-element.20.f_ref, f32[4,5,4,640]{3,2,1,0:T(4,128)S(1)} %get-tuple-element.21.p_ref, s32[1,640]{1,0:T(1,128)S(1)} %broadcast_in_dim.3.folds_ref), custom_call_target="tpu_custom_call" | custom-call | tf_op jit(solution)/shard_map/blend/pallas_call | solution.py:787
Async XLA Ops:
  1.3 1.1 copy-start
  2.4 0.7 copy-start.2
  3.1 113.2 %copy-start.1 = (bf16[640,512]{1,0:T(8,128)(2,1)S(1)}, bf16[640,512]{1,0:T(8,128)(2,1)}, u32[]{:S(2)}) copy-start(bf16[640,512]{1,0:T(8,128)(2,1)} %x_ref.3) | copy-start | bytes 1966084
